TPU v7x, 512 devices: a whole 4x4x16 slice. The times are simulated.
512 devices in a mesh: replica: 32 (over x, z_hi, y), fsdp: 16 (over z_lo, core).
Axes of the slice: x: 4, y: 4, z: 16 (z_hi: 2, z_lo: 8; z = z_hi * 8 + z_lo), core: 2. Of those that a mesh axis runs over, the one named last changes fastest.
Arguments:
- features: bfloat16 [32, 3072, 2048], P('replica', 'fsdp'), may hold values from -6 to 6
- cotangent: bfloat16 [32, 3072, 2048], P('replica', 'fsdp'), may hold values from -6 to 6
- master: float32 [32, 2048, 2048], P('replica', None, 'fsdp'), may hold values from -0.75 to 0.75
- moment: bfloat16 [32, 2048, 2048], P('replica', None, 'fsdp'), may hold values from -6 to 6
- variance: float32 [32, 2048, 2048], P('replica', None, 'fsdp'), may hold values from 0.05 to 1
- step_count: int32 [1], replicated, may hold values from 1 to 24
Outputs:
- mixed: float32 [32, 2048, 2048], P('replica', None, 'fsdp')
All inputs are finite; a program needn't handle non-finite values.
Results may differ from a plain program's by a relative error of at most 0.0022.
Values may be sent and summed in bfloat16 or wider, within the bound.
No kernel may reach another device: no remote copies, remote signals or barrier semaphores. Data moves between devices by JAX's collectives and lax.ppermute only.
A program may use at most 64 MiB of HBM per device.

v0:
```python
from functools import partial

import jax
import jax.numpy as jnp
from jax import lax
from jax.sharding import PartitionSpec as P

D_IN = 2048
HEAD = 128


def passed_along(value, axis, steps):
    count = lax.axis_size(axis)
    pairs = [(source, (source + steps) % count) for source in range(count)]
    return lax.ppermute(value, axis, pairs)


def head_gradient(tokens, weights, cotangent, heads_here):
    scale = D_IN ** (-0.5)
    query = jnp.dot(tokens, weights, preferred_element_type=jnp.float32) * scale
    count_rows = query.shape[0]
    shaped = query.reshape(count_rows, heads_here, HEAD)
    inverse = lax.rsqrt(jnp.mean(shaped * shaped, axis=-1, keepdims=True) + 1e-06)
    normed = shaped * inverse
    upstream = cotangent.astype(jnp.float32).reshape(count_rows, heads_here, HEAD)
    projected = jnp.mean(upstream * normed, axis=-1, keepdims=True)
    dquery = (
        (inverse * (upstream - normed * projected))
        .reshape(count_rows, heads_here * HEAD)
        .astype(jnp.bfloat16)
    )
    return lax.dot_general(
        tokens, dquery, (((0,), (0,)), ((), ())), preferred_element_type=jnp.float32
    )


def pull_fresh(value, distance):
    return passed_along(value, "replica", distance)


def body(features, cotangent, master, moment, variance, step_count):
    counter = step_count[0]
    selector = counter % 4
    params = master[0]
    tokens = features[0]
    local_cols = params.shape[1]
    heads_here = local_cols // HEAD
    columns = lax.all_to_all(cotangent[0], "fsdp", split_axis=1, concat_axis=0, tiled=True)
    weights = params.astype(jnp.bfloat16)
    gathered = lax.all_gather(tokens, "fsdp", axis=0, tiled=True)
    summed = head_gradient(gathered, weights, columns, heads_here)
    grads = summed * D_IN ** (-0.5)
    power = counter.astype(jnp.float32)
    correct_first = 1.0 - jnp.power(jnp.float32(0.9), power)
    correct_second = 1.0 - jnp.power(jnp.float32(0.999), power)
    first = 0.9 * moment[0].astype(jnp.float32) + 0.1 * grads
    second = 0.999 * variance[0] + 0.001 * grads * grads
    update = 0.1 * (
        first / correct_first / (jnp.sqrt(second / correct_second) + 1e-08) + 0.1 * params
    )
    fresh = params - update
    received = lax.switch(
        selector, [partial(pull_fresh, distance=1 << level) for level in range(4)], fresh
    )
    return (0.5 * (fresh + received))[None]


def solution(mesh):
    placed = (
        P("replica", "fsdp", None),
        P("replica", "fsdp", None),
        P("replica", None, "fsdp"),
        P("replica", None, "fsdp"),
        P("replica", None, "fsdp"),
        P(),
    )
    return jax.shard_map(
        body, mesh=mesh, in_specs=placed, out_specs=P("replica", None, "fsdp"), check_vma=False
    )
```

profile of v0, /device:TPU:113, one launch (start us, length us, event | category | flops | bytes accessed | tf_op | source)
XLA Modules:
  0.0 234.9 jit_solution(16718094906365795572)
XLA Ops:
  6.5 0.0 all-gather.3.cloned.1.call-start
  6.5 0.7 all-gather.3.cloned.1.call-update
  7.3 1.3 copy.60
  8.6 0.0 copy-start
  8.6 1.2 copy.42
  9.7 0.0 copy-start.1
  9.7 12.2 %all-to-all-start = ((bf16[192,16,128]{2,0,1:T(8,128)(2,1)}), bf16[192,16,128]{2,0,1:T(8,128)(2,1)S(1)}, u32[]{:S(2)}, u32[]{:S(2)}) async-start(bf16[192,16,128]{2,0,1:T(8,128)(2,1)} %copy.42), calls=%async_computation | async-start | bytes 1572864 | tf_op jit(solution)/shard_map/all_to_all | solution.py:48
  22.6 0.0 copy-done
  22.6 1.3 copy.40
  23.9 0.0 copy-start.5
  24.0 0.0 copy-done.1
  24.0 1.3 copy.45
  25.3 0.0 copy-done.5
  25.3 0.2 copy.41
  25.5 56.9 %all-to-all-done = bf16[192,16,128]{2,0,1:T(8,128)(2,1)S(1)} async-done(((bf16[192,16,128]{2,0,1:T(8,128)(2,1)}), bf16[192,16,128]{2,0,1:T(8,128)(2,1)S(1)}, u32[]{:S(2)}, u32[]{:S(2)}) %all-to-all-start) | async-done | bytes 786464 | tf_op jit(solution)/shard_map/all_to_all | solution.py:48
  82.4 1.3 convert_element_type.30
  83.7 0.0 copy-start.2
  83.7 2.0 copy.44
  85.7 100.8 %all-gather.3.cloned.1.call-done = bf16[1,3072,2048]{2,1,0:T(8,128)(2,1)} async-done(((bf16[1,192,2048]{2,1,0:T(8,128)(2,1)}), bf16[1,3072,2048]{2,1,0:T(8,128)(2,1)}) %all-gather.3.cloned.1.call-update) | async-done | bytes 12582928 | tf_op jit(solution)/shard_map/all_gather | solution.py:50
  186.5 0.0 copy-done.2
  186.5 0.0 copy-start.6
  186.5 9.0 %multiply_reduce_fusion.1 = (f32[3072]{0:T(1024)S(1)}, f32[3072,128]{0,1:T(8,128)S(1)}) fusion(bf16[1,3072,2048]{2,1,0:T(8,128)(2,1)} %all-gather.3.cloned.1.call-done, f32[1,2048,128]{1,2,0:T(8,128)S(1)} %copy-done.2), kind=kOutput, calls=%fused_computation.6 | convolution fusion | flops 1611789312 | bytes 15216640 | tf_op jit(solution)/shard_map/dot_general | solution.py:20
  195.5 0.0 copy-start.3
  195.5 0.0 copy-start.4
  195.5 0.3 multiply_reduce_fusion
  195.8 0.0 copy-done.6
  195.8 0.9 copy-done.3
  196.8 0.3 copy-done.4
  197.1 3.0 %bitcast_subtract_fusion = f32[2048,128]{0,1:T(8,128)S(1)} fusion(f32[1,2048,128]{1,2,0:T(8,128)S(1)} %copy-done.3, f32[1,2048,128]{1,2,0:T(8,128)S(1)} %copy-done.4, bf16[1,3072,2048]{2,1,0:T(8,128)(2,1)S(1)} %copy-done.6, bf16[1,2048,128]{1,2,0:T(8,128)(2,1)S(1)} %copy.41, f32[3072,128]{0,1:T(8,128)S(1)} %copy.44, f32[3072,128]{0,1:T(8,128)S(1)} %get-tuple-element.22, ...), kind=kOutput, calls=%fused_computation.15 | convolution fusion | flops 1617035264 | bytes 19435528 | tf_op jit(solution)/shard_map/dot_general | solution.py:32
  200.0 26.5 %conditional.1 = (f32[2048,128]{0,1:T(8,128)S(1)}) conditional(s32[]{:T(128)} %clamp.3, (f32[2048,128]{0,1:T(8,128)S(1)}) %tuple.21, (f32[2048,128]{0,1:T(8,128)S(1)}) %tuple.21, (f32[2048,128]{0,1:T(8,128)S(1)}) %tuple.21, (f32[2048,128]{0,1:T(8,128)S(1)}) %tuple.21), branch_computations={%region_2.3_spmd, %region_3.4_spmd, %region_4.5_spmd, %region_5.6_... | conditional | bytes 8388656 | solution.py:62
  200.1 0.3 copy.59
  200.4 3.1 %collective-permute-start.3 = (f32[2048,128]{1,0:T(8,128)S(1)}, f32[2048,128]{1,0:T(8,128)S(1)}, u32[]{:S(2)}, u32[]{:S(2)}) collective-permute-start(f32[2048,128]{1,0:T(8,128)S(1)} %copy.59), channel_id=1, source_target_pairs={{0,128},{16,144},{32,160},{48,176},{64,192},{80,208},{96,224},{112... | collective-permute-start | bytes 3145736 | tf_op jit(solution)/shard_map/cond/branch_3_fun/ppermute | solution.py:15
  203.5 22.7 %collective-permute-done.3 = f32[2048,128]{1,0:T(8,128)S(1)} collective-permute-done((f32[2048,128]{1,0:T(8,128)S(1)}, f32[2048,128]{1,0:T(8,128)S(1)}, u32[]{:S(2)}, u32[]{:S(2)}) %collective-permute-start.3) | collective-permute-done | bytes 1048608 | tf_op jit(solution)/shard_map/cond/branch_3_fun/ppermute | solution.py:15
  226.3 0.3 copy.55
  226.6 0.1 multiply_bitcast_fusion
  226.7 1.3 copy.51
  (2 shorter events, 0.0 us)
Async XLA Ops:
  6.5 180.0 %all-gather.3.cloned.1.call-start = ((), (), s32[]{:S(2)}) async-start(), calls=%async_computation.1 | async-start | bytes 13369344 | tf_op jit(solution)/shard_map/all_gather | solution.py:50
  8.6 14.0 %copy-start = (f32[1,2048,128]{2,1,0:T(8,128)S(1)}, f32[1,2048,128]{2,1,0:T(8,128)}, u32[]{:S(2)}) copy-start(f32[1,2048,128]{2,1,0:T(8,128)} %param.12) | copy-start | bytes 3145732
  9.7 14.3 %copy-start.1 = (f32[1,2048,128]{2,1,0:T(8,128)S(1)}, f32[1,2048,128]{2,1,0:T(8,128)}, u32[]{:S(2)}) copy-start(f32[1,2048,128]{2,1,0:T(8,128)} %param.14) | copy-start | bytes 3145732
  9.7 72.7 %all-to-all-start = ((bf16[192,16,128]{2,0,1:T(8,128)(2,1)}), bf16[192,16,128]{2,0,1:T(8,128)(2,1)S(1)}, u32[]{:S(2)}, u32[]{:S(2)}) async-start(bf16[192,16,128]{2,0,1:T(8,128)(2,1)} %copy.42), calls=%async_computation | async-start | bytes 1572864 | tf_op jit(solution)/shard_map/all_to_all | solution.py:48
  23.9 1.4 copy-start.5
  83.7 102.8 %copy-start.2 = (f32[1,2048,128]{1,2,0:T(8,128)S(1)}, f32[1,2048,128]{1,2,0:T(8,128)}, u32[]{:S(2)}) copy-start(f32[1,2048,128]{1,2,0:T(8,128)} %copy.40) | copy-start | bytes 3145732
  186.5 9.3 %copy-start.6 = (bf16[1,3072,2048]{2,1,0:T(8,128)(2,1)S(1)}, bf16[1,3072,2048]{2,1,0:T(8,128)(2,1)}, u32[]{:S(2)}) copy-start(bf16[1,3072,2048]{2,1,0:T(8,128)(2,1)} %all-gather.3.cloned.1.call-done) | copy-start | bytes 37748740
  195.5 1.2 copy-start.3
  195.5 1.5 copy-start.4
  200.4 25.8 %collective-permute-start.3 = (f32[2048,128]{1,0:T(8,128)S(1)}, f32[2048,128]{1,0:T(8,128)S(1)}, u32[]{:S(2)}, u32[]{:S(2)}) collective-permute-start(f32[2048,128]{1,0:T(8,128)S(1)} %copy.59), channel_id=1, source_target_pairs={{0,128},{16,144},{32,160},{48,176},{64,192},{80,208},{96,224},{112... | collective-permute-start | bytes 3145736 | tf_op jit(solution)/shard_map/cond/branch_3_fun/ppermute | solution.py:15
Sparse Core Ops, SparseCore 0:
  9.4 177.0 all-gather.2
where the time goes:
time: 235 us
  waiting for transfers between devices  181 us (77%)
  starting transfers between devices  15.3 us (7%)
  between operations  14.3 us (6%)
  matrix products  12 us (5%)
  local copies, waits for them, and re-layouts  10.5 us (4%)
    all_gather x1, waiting for transfers between devices, body(): gathered = lax.all_gather(tokens, 'fsdp', axis=0, tiled=True)  101 us
    all_to_all x1, waiting for transfers between devices, body(): lax.all_to_all(cotangent[0], 'fsdp', split_axis=1, concat_axis=0, tiled=T...  56.9 us
    ppermute x1, waiting for transfers between devices, passed_along(): return lax.ppermute(value, axis, pairs)  22.7 us
    all_to_all x1, starting transfers between devices, body(): lax.all_to_all(cotangent[0], 'fsdp', split_axis=1, concat_axis=0, tiled=T...  12.2 us
    dot_general x1, matrix products, head_gradient(): query = jnp.dot(tokens, weights, preferred_element_type=jnp.float32) * scale  9 us
    unnamed x18, local copies, waits for them, and re-layouts  5.37 us
  transfers between devices with their start and end apart: 3, of which 3 were waited for; matrix products, arithmetic and copies ran while one was open for 4% of the time, Pallas kernels for 0%

commit v1 on v0

v1 whole, which is shorter than its diff:
```python
from functools import partial

import jax
import jax.numpy as jnp
from jax import lax
from jax.experimental import pallas as pl
from jax.experimental.pallas import tpu as pltpu
from jax.sharding import PartitionSpec as P

D_IN = 2048
HEAD = 128
CORES = 2
ROWS = 512


def gradient_kernel(info, x_ref, w_ref, cot_ref, own_in, other_in, own_out, other_out):
    valid, block, core = info[0], info[1], info[2]

    @pl.when(valid > 0)
    def _():
        x = x_ref[...]
        query = jnp.dot(x, w_ref[...], preferred_element_type=jnp.float32) * D_IN ** (-0.5)
        cot = cot_ref[block].astype(jnp.float32)
        first, second = cot[:, :HEAD], cot[:, HEAD:]
        upstreams = (
            jnp.where(core == 0, first, second),
            jnp.where(core == 0, second, first),
        )
        parts = []
        for at, upstream in enumerate(upstreams):
            shaped = query[:, at * HEAD : (at + 1) * HEAD]
            inverse = lax.rsqrt(jnp.mean(shaped * shaped, axis=-1, keepdims=True) + 1e-06)
            normed = shaped * inverse
            projected = jnp.mean(upstream * normed, axis=-1, keepdims=True)
            parts.append((inverse * (upstream - normed * projected)).astype(jnp.bfloat16))
        dquery = jnp.concatenate(parts, axis=1)
        for at in range(0, D_IN, ROWS):
            rows = slice(at, at + ROWS)
            part = lax.dot_general(
                x_ref[:, rows], dquery, (((0,), (0,)), ((), ())), preferred_element_type=jnp.float32
            )
            own_out[rows, :] = own_in[rows, :] + part[:, :HEAD]
            other_out[rows, :] = other_in[rows, :] + part[:, HEAD:]


def accumulate(sums, x, weights, cots, valid, block, core):
    info = jnp.stack([valid, block, core]).astype(jnp.int32)
    vmem = pl.BlockSpec(memory_space=pltpu.VMEM)
    tokens = x.shape[0]
    return pl.pallas_call(
        gradient_kernel,
        out_shape=[jax.ShapeDtypeStruct(s.shape, s.dtype) for s in sums],
        in_specs=[pl.BlockSpec(memory_space=pltpu.SMEM)] + [vmem] * 5,
        out_specs=[vmem, vmem],
        input_output_aliases={4: 0, 5: 1},
        cost_estimate=pl.CostEstimate(
            flops=8 * tokens * D_IN * HEAD, bytes_accessed=6 * 2**20, transcendentals=2 * tokens
        ),
        compiler_params=pltpu.CompilerParams(vmem_limit_bytes=32 * 2**20),
    )(info, x, weights, cots, *sums)


def chip_pairs(chips, sources, step):
    return [
        (chip * CORES + core, (chip + step) * CORES + core)
        for chip in sources
        for core in range(CORES)
        if 0 <= chip + step < chips
    ]


def pull_fresh(value, distance):
    count = lax.axis_size("replica")
    pairs = [(source, (source + distance) % count) for source in range(count)]
    return lax.ppermute(value, "replica", pairs)


def body(features, cotangent, master, moment, variance, step_count):
    counter = step_count[0]
    selector = counter % 4
    params = master[0]
    tokens = features[0]
    devices = lax.axis_size("fsdp")
    chips = devices // CORES
    half = chips // 2
    index = lax.axis_index("fsdp")
    chip, core = index // CORES, index % CORES
    rows = tokens.shape[0]

    def hop(value, sources, step):
        return lax.ppermute(value, "fsdp", chip_pairs(chips, sources, step))

    groups = [[at * CORES + c for at in range(chips)] for c in range(CORES)]
    cots = lax.all_to_all(
        cotangent[0].reshape(rows, chips, CORES * HEAD).transpose(1, 0, 2),
        "fsdp",
        split_axis=0,
        concat_axis=0,
        axis_index_groups=groups,
    )
    weights = params.astype(jnp.bfloat16)
    swapped = [(at, at ^ 1) for at in range(devices)]
    weights = jnp.concatenate([weights, lax.ppermute(weights, "fsdp", swapped)], axis=1)

    arrived = [(tokens, jnp.int32(1), chip)]
    right = left = tokens
    for step in range(1, half + 1):
        right = hop(right, range(step - 1, chips), 1)
        left = hop(left, range(0, chips - step + 1), -1)
        if step < half:
            arrived.append((right, chip >= step, chip - step))
            arrived.append((left, chip < chips - step, chip + step))
    upper = chip >= half
    block = jnp.where(upper, right, left)
    for step in range(half, chips):
        if step > half:
            pairs = chip_pairs(chips, range(step - 1, chips), 1)
            pairs += chip_pairs(chips, range(0, chips - step + 1), -1)
            block = lax.ppermute(block, "fsdp", pairs)
        valid = jnp.where(upper, chip >= step, chip < chips - step)
        arrived.append((block, valid, jnp.where(upper, chip - step, chip + step)))

    sums = [jnp.zeros((D_IN, HEAD), jnp.float32)] * 2
    for x, valid, source in arrived:
        sums = accumulate(
            sums, x, weights, cots, valid, jnp.clip(source, 0, chips - 1), core
        )
    own, other = sums
    summed = own + lax.ppermute(other, "fsdp", swapped)

    grads = summed * D_IN ** (-0.5)
    power = counter.astype(jnp.float32)
    correct_first = 1.0 - jnp.power(jnp.float32(0.9), power)
    correct_second = 1.0 - jnp.power(jnp.float32(0.999), power)
    first = 0.9 * moment[0].astype(jnp.float32) + 0.1 * grads
    second = 0.999 * variance[0] + 0.001 * grads * grads
    update = 0.1 * (
        first / correct_first / (jnp.sqrt(second / correct_second) + 1e-08) + 0.1 * params
    )
    fresh = params - update
    received = lax.switch(
        selector,
        [partial(pull_fresh, distance=1 << level) for level in range(4)],
        fresh.astype(jnp.bfloat16),
    )
    return (0.5 * (fresh + received.astype(jnp.float32)))[None]


def solution(mesh):
    placed = (
        P("replica", "fsdp", None),
        P("replica", "fsdp", None),
        P("replica", None, "fsdp"),
        P("replica", None, "fsdp"),
        P("replica", None, "fsdp"),
        P(),
    )
    return jax.shard_map(
        body, mesh=mesh, in_specs=placed, out_specs=P("replica", None, "fsdp"), check_vma=False
    )
```

time: 235 us -> 207 us (0.88)
  the two profiles are of different devices: /device:TPU:113 before, /device:TPU:48 now
where the time goes in v1:
time: 207 us; the launch traced here: 206 us
  waiting for transfers between devices  124 us (60%)
  starting transfers between devices  44 us (21%)
  Pallas kernels  18.9 us (9%)
  local copies, waits for them, and re-layouts  10.2 us (5%)
  other arithmetic  7.18 us (3%)
    ppermute x3, waiting for transfers between devices, body(): block = lax.ppermute(block, 'fsdp', pairs)  56.5 us
    ppermute x8, waiting for transfers between devices, hop(): return lax.ppermute(value, 'fsdp', chip_pairs(chips, sources, step))  51.9 us
    pallas_call x11, Pallas kernels, accumulate(): pl.pallas_call(gradient_kernel, out_shape=[jax.ShapeDtypeStruct(s.shape,...  18.9 us
    ppermute x8, starting transfers between devices, hop(): return lax.ppermute(value, 'fsdp', chip_pairs(chips, sources, step))  17.9 us
    ppermute x1, waiting for transfers between devices, pull_fresh(): return lax.ppermute(value, 'replica', pairs)  13.8 us
    all_to_all x1, starting transfers between devices, body(): lax.all_to_all(cotangent[0].reshape(rows, chips, CORES * HEAD).transpose(...  12.8 us
    unnamed x41, local copies, waits for them, and re-layouts  9.02 us
    ppermute x3, starting transfers between devices, body(): block = lax.ppermute(block, 'fsdp', pairs)  6.08 us
  transfers between devices with their start and end apart: 15, of which 8 were waited for; matrix products, arithmetic and copies ran while one was open for 2% of the time, Pallas kernels for 9%

profile of v1, /device:TPU:48, one launch (start us, length us, event | category | flops | bytes accessed | tf_op | source)
XLA Modules:
  0.0 205.8 jit_solution(2145748564885767918)
XLA Ops:
  0.0 2.0 collective-permute-start.8
  2.0 3.8 %collective-permute-start.4 = (bf16[192,2048]{1,0:T(8,128)(2,1)}, bf16[192,2048]{1,0:T(8,128)(2,1)S(1)}, u32[]{:S(2)}, u32[]{:S(2)}) collective-permute-start(bf16[192,2048]{1,0:T(8,128)(2,1)} %bitcast.70), channel_id=1, source_target_pairs={{0,2},{1,3},{2,4},{3,5},{4,6},{5,7},{6,8},{7,9},{8,10},{9,11},{10,... | collective-permute-start | bytes 2359304 | tf_op jit(solution)/shard_map/ppermute | solution.py:91
  5.9 15.7 %collective-permute-done.8.x_ref = bf16[192,2048]{1,0:T(8,128)(2,1)S(1)} collective-permute-done((bf16[192,2048]{1,0:T(8,128)(2,1)}, bf16[192,2048]{1,0:T(8,128)(2,1)S(1)}, u32[]{:S(2)}, u32[]{:S(2)}) %collective-permute-start.8) | collective-permute-done | bytes 786464 | tf_op jit(solution)/shard_map/ppermute | solution.py:91
  21.6 2.0 collective-permute-start.9
  23.6 0.9 copy-done.9
  24.5 3.9 %collective-permute-start.5 = (bf16[192,2048]{1,0:T(8,128)(2,1)S(1)}, bf16[192,2048]{1,0:T(8,128)(2,1)S(1)}, u32[]{:S(2)}, u32[]{:S(2)}) collective-permute-start(bf16[192,2048]{1,0:T(8,128)(2,1)S(1)} %collective-permute-done.4.x_ref), channel_id=1, source_target_pairs={{2,4},{3,5},{4,6},{5,7},{6,8},{7,9},{8,10},{9,11},{10,12},{11,13},... | collective-permute-start | bytes 2359304 | tf_op jit(solution)/shard_map/ppermute | solution.py:91
  28.3 0.9 copy-done.15
  29.2 13.0 %collective-permute-done.9.x_ref = bf16[192,2048]{1,0:T(8,128)(2,1)S(1)} collective-permute-done((bf16[192,2048]{1,0:T(8,128)(2,1)S(1)}, bf16[192,2048]{1,0:T(8,128)(2,1)S(1)}, u32[]{:S(2)}, u32[]{:S(2)}) %collective-permute-start.9) | collective-permute-done | bytes 786464 | tf_op jit(solution)/shard_map/ppermute | solution.py:91
  42.2 2.0 collective-permute-start.10
  44.3 0.9 copy-done.7
  45.2 0.7 collective-permute-start.6
  45.9 0.9 copy-done.13
  46.8 16.7 %collective-permute-done.10.x_ref = bf16[192,2048]{1,0:T(8,128)(2,1)S(1)} collective-permute-done((bf16[192,2048]{1,0:T(8,128)(2,1)S(1)}, bf16[192,2048]{1,0:T(8,128)(2,1)S(1)}, u32[]{:S(2)}, u32[]{:S(2)}) %collective-permute-start.10) | collective-permute-done | bytes 786464 | tf_op jit(solution)/shard_map/ppermute | solution.py:91
  63.5 1.9 collective-permute-start.11
  65.4 1.6 collective-permute-start.7
  67.0 1.3 copy.30
  68.3 1.0 copy.32
  69.4 12.8 %all-to-all-start = ((bf16[8,192,256]{2,1,0:T(8,128)(2,1)}), bf16[8,192,256]{2,1,0:T(8,128)(2,1)S(1)}, u32[]{:S(2)}, u32[]{:S(2)}) async-start(bf16[8,192,256]{2,1,0:T(8,128)(2,1)} %bitcast.64), calls=%async_computation | async-start | bytes 1572864 | tf_op jit(solution)/shard_map/all_to_all | solution.py:94
  82.2 6.4 %collective-permute-done.11 = bf16[192,2048]{1,0:T(8,128)(2,1)S(1)} collective-permute-done((bf16[192,2048]{1,0:T(8,128)(2,1)S(1)}, bf16[192,2048]{1,0:T(8,128)(2,1)S(1)}, u32[]{:S(2)}, u32[]{:S(2)}) %collective-permute-start.11) | collective-permute-done | bytes 786464 | tf_op jit(solution)/shard_map/ppermute | solution.py:91
  88.8 1.9 collective-permute-start.12
  90.8 1.9 collective-permute-start.15
  92.9 32.6 %collective-permute-done.12.x_ref = bf16[192,2048]{1,0:T(8,128)(2,1)S(1)} collective-permute-done((bf16[192,2048]{1,0:T(8,128)(2,1)S(1)}, bf16[192,2048]{1,0:T(8,128)(2,1)S(1)}, u32[]{:S(2)}, u32[]{:S(2)}) %collective-permute-start.12) | collective-permute-done | bytes 786464 | tf_op jit(solution)/shard_map/ppermute | solution.py:119
  125.5 1.9 collective-permute-start.13
  127.4 0.9 copy-done.17
  128.8 23.9 %collective-permute-done.13.x_ref = bf16[192,2048]{1,0:T(8,128)(2,1)} collective-permute-done((bf16[192,2048]{1,0:T(8,128)(2,1)S(1)}, bf16[192,2048]{1,0:T(8,128)(2,1)}, u32[]{:S(2)}, u32[]{:S(2)}) %collective-permute-start.13) | collective-permute-done | bytes 786464 | tf_op jit(solution)/shard_map/ppermute | solution.py:119
  152.8 2.2 %collective-permute-start.14 = (bf16[192,2048]{1,0:T(8,128)(2,1)}, bf16[192,2048]{1,0:T(8,128)(2,1)}, u32[]{:S(2)}, u32[]{:S(2)}) collective-permute-start(bf16[192,2048]{1,0:T(8,128)(2,1)} %collective-permute-done.13.x_ref), channel_id=1, source_target_pairs={{12,14},{13,15},{2,0},{3,1},{28,30},{29,31},{18,16},{19,17},{44,46... | collective-permute-start | bytes 2359304 | tf_op jit(solution)/shard_map/ppermute | solution.py:119
  155.2 1.2 pad_maximum_fusion.w_ref
  156.3 0.9 copy-done
  157.4 1.0 copy-done.4
  158.6 2.0 shard_map.64
  160.6 2.0 shard_map.65
  162.6 2.0 shard_map.66
  164.6 0.6 shard_map.67
  165.2 0.6 copy-done.8
  165.8 2.0 shard_map.68
  168.3 0.6 copy-done.6
  168.9 2.0 shard_map.70
  170.9 2.0 shard_map.71
  172.9 2.2 %shard_map.72 = (f32[2048,128]{1,0:T(8,128)S(1)}, f32[2048,128]{1,0:T(8,128)S(1)}) custom-call(s32[3]{0:T(128)S(1)} %add_add_fusion.2.info, bf16[192,2048]{1,0:T(8,128)(2,1)S(1)} %copy-done.18, bf16[2048,256]{1,0:T(8,128)(2,1)S(1)} %pad_maximum_fusion.w_ref, bf16[8,192,256]{2,1,0:T(8,128)(2,1)S(1)} %copy-done.1, ...), custom_call_target="tpu_custom_call", output_to_operand_aliasing={{0}: (4, {}), {1}: (5, {})} | custom-call | flops 402653184 | bytes 6291456 | tf_op jit(solution)/shard_map/pallas_call | solution.py:50
  175.1 2.6 %shard_map.73 = (f32[2048,128]{1,0:T(8,128)S(1)}, f32[2048,128]{1,0:T(8,128)S(1)}) custom-call(s32[3]{0:T(128)S(1)} %add_add_fusion.1.info, bf16[192,2048]{1,0:T(8,128)(2,1)} %collective-permute-done.13.x_ref, bf16[2048,256]{1,0:T(8,128)(2,1)S(1)} %pad_maximum_fusion.w_ref, ...), custom_call_target="tpu_custom_call", output_to_operand_aliasing={{0}: (4, {}), {1}: (5, {})} | custom-call | flops 402653184 | bytes 6291456 | tf_op jit(solution)/shard_map/pallas_call | solution.py:50
  177.7 1.2 shard_map.74
  178.8 1.9 collective-permute-start.16
  181.5 2.0 collective-permute-done.16
  183.5 2.9 %fusion.6 = (bf16[2048,128]{1,0:T(8,128)(2,1)S(1)}, f32[2048,128]{1,0:T(8,128)S(1)}) fusion(f32[]{:T(128)S(6)} %sub.43, f32[1,2048,128]{2,1,0:T(8,128)} %param.14, f32[]{:T(128)S(6)} %sub.42, f32[2048,128]{1,0:T(8,128)S(1)} %get-tuple-element.62, f32[2048,128]{1,0:T(8,128)} %collective-permute-done.16, bf16[1,2048,128]{2,1,0:T(8,128)(2,1)} %param.13, ...), kind=kLoop, calls=%fused_computation.26 | loop fusion | flops 4980736 | bytes 6291464 | tf_op jit(solution)/shard_map/convert_element_type | solution.py:144
  186.5 17.2 %conditional.4 = (bf16[2048,128]{1,0:T(8,128)(2,1)}) conditional(s32[]{:T(128)} %clamp.3, bf16[2048,128]{1,0:T(8,128)(2,1)S(1)} %get-tuple-element.64, bf16[2048,128]{1,0:T(8,128)(2,1)S(1)} %get-tuple-element.64, bf16[2048,128]{1,0:T(8,128)(2,1)S(1)} %get-tuple-element.64, ...), branch_computations={%region_0.1_spmd, %region_1.2_spmd, %region_2.3_spmd, %region_3.4_... | conditional | bytes 2097200
  186.5 3.4 %collective-permute-start.3 = (bf16[2048,128]{1,0:T(8,128)(2,1)S(1)}, bf16[2048,128]{1,0:T(8,128)(2,1)}, u32[]{:S(2)}, u32[]{:S(2)}) collective-permute-start(bf16[2048,128]{1,0:T(8,128)(2,1)S(1)} %param.3), channel_id=1, source_target_pairs={{0,128},{16,144},{32,160},{48,176},{64,192},{80,208},{96,224},{112... | collective-permute-start | bytes 1572872 | tf_op jit(solution)/shard_map/cond/branch_3_fun/ppermute | solution.py:75
  189.9 13.8 %collective-permute-done.3 = bf16[2048,128]{1,0:T(8,128)(2,1)} collective-permute-done((bf16[2048,128]{1,0:T(8,128)(2,1)S(1)}, bf16[2048,128]{1,0:T(8,128)(2,1)}, u32[]{:S(2)}, u32[]{:S(2)}) %collective-permute-start.3) | collective-permute-done | bytes 524320 | tf_op jit(solution)/shard_map/cond/branch_3_fun/ppermute | solution.py:75
  203.7 2.1 %multiply_bitcast_fusion = f32[1,2048,128]{2,1,0:T(8,128)} fusion(f32[2048,128]{1,0:T(8,128)S(1)} %get-tuple-element.65, bf16[2048,128]{1,0:T(8,128)(2,1)} %get-tuple-element.66), kind=kLoop, calls=%fused_computation.12 | loop fusion | flops 786432 | bytes 2621440 | tf_op jit(solution)/shard_map/broadcast_in_dim | solution.py:146
  (54 shorter events, 2.0 us)
Async XLA Ops:
  0.0 21.6 %collective-permute-start.8 = (bf16[192,2048]{1,0:T(8,128)(2,1)}, bf16[192,2048]{1,0:T(8,128)(2,1)S(1)}, u32[]{:S(2)}, u32[]{:S(2)}) collective-permute-start(bf16[192,2048]{1,0:T(8,128)(2,1)} %bitcast.69), channel_id=1, source_target_pairs={{2,0},{3,1},{4,2},{5,3},{6,4},{7,5},{8,6},{9,7},{10,8},{11,9},{12,... | collective-permute-start | bytes 2359304 | tf_op jit(solution)/shard_map/ppermute | solution.py:91
  2.0 22.5 %collective-permute-start.4 = (bf16[192,2048]{1,0:T(8,128)(2,1)}, bf16[192,2048]{1,0:T(8,128)(2,1)S(1)}, u32[]{:S(2)}, u32[]{:S(2)}) collective-permute-start(bf16[192,2048]{1,0:T(8,128)(2,1)} %bitcast.70), channel_id=1, source_target_pairs={{0,2},{1,3},{2,4},{3,5},{4,6},{5,7},{6,8},{7,9},{8,10},{9,11},{10,... | collective-permute-start | bytes 2359304 | tf_op jit(solution)/shard_map/ppermute | solution.py:91
  21.6 20.7 %collective-permute-start.9 = (bf16[192,2048]{1,0:T(8,128)(2,1)S(1)}, bf16[192,2048]{1,0:T(8,128)(2,1)S(1)}, u32[]{:S(2)}, u32[]{:S(2)}) collective-permute-start(bf16[192,2048]{1,0:T(8,128)(2,1)S(1)} %collective-permute-done.8.x_ref), channel_id=1, source_target_pairs={{2,0},{3,1},{4,2},{5,3},{6,4},{7,5},{8,6},{9,7},{10,8},{11,9},{12,... | collective-permute-start | bytes 2359304 | tf_op jit(solution)/shard_map/ppermute | solution.py:91
  23.6 0.9 copy-start.9
  24.5 20.7 %collective-permute-start.5 = (bf16[192,2048]{1,0:T(8,128)(2,1)S(1)}, bf16[192,2048]{1,0:T(8,128)(2,1)S(1)}, u32[]{:S(2)}, u32[]{:S(2)}) collective-permute-start(bf16[192,2048]{1,0:T(8,128)(2,1)S(1)} %collective-permute-done.4.x_ref), channel_id=1, source_target_pairs={{2,4},{3,5},{4,6},{5,7},{6,8},{7,9},{8,10},{9,11},{10,12},{11,13},... | collective-permute-start | bytes 2359304 | tf_op jit(solution)/shard_map/ppermute | solution.py:91
  28.3 0.9 copy-start.15
  42.2 21.3 %collective-permute-start.10 = (bf16[192,2048]{1,0:T(8,128)(2,1)S(1)}, bf16[192,2048]{1,0:T(8,128)(2,1)S(1)}, u32[]{:S(2)}, u32[]{:S(2)}) collective-permute-start(bf16[192,2048]{1,0:T(8,128)(2,1)S(1)} %collective-permute-done.9.x_ref), channel_id=1, source_target_pairs={{2,0},{3,1},{4,2},{5,3},{6,4},{7,5},{8,6},{9,7},{10,8},{11,9},{18,... | collective-permute-start | bytes 2359304 | tf_op jit(solution)/shard_map/ppermute | solution.py:91
  44.3 0.9 copy-start.7
  45.2 20.3 %collective-permute-start.6 = (bf16[192,2048]{1,0:T(8,128)(2,1)S(1)}, bf16[192,2048]{1,0:T(8,128)(2,1)S(1)}, u32[]{:S(2)}, u32[]{:S(2)}) collective-permute-start(bf16[192,2048]{1,0:T(8,128)(2,1)S(1)} %collective-permute-done.5.x_ref), channel_id=1, source_target_pairs={{4,6},{5,7},{6,8},{7,9},{8,10},{9,11},{10,12},{11,13},{12,14},{13,... | collective-permute-start | bytes 2359304 | tf_op jit(solution)/shard_map/ppermute | solution.py:91
  45.9 0.9 copy-start.13
  63.5 5.9 %copy-start.5 = (bf16[192,2048]{1,0:T(8,128)(2,1)}, bf16[192,2048]{1,0:T(8,128)(2,1)S(1)}, u32[]{:S(2)}) copy-start(bf16[192,2048]{1,0:T(8,128)(2,1)S(1)} %collective-permute-done.10.x_ref) | copy-start | bytes 2359300
  63.5 25.2 %collective-permute-start.11 = (bf16[192,2048]{1,0:T(8,128)(2,1)S(1)}, bf16[192,2048]{1,0:T(8,128)(2,1)S(1)}, u32[]{:S(2)}, u32[]{:S(2)}) collective-permute-start(bf16[192,2048]{1,0:T(8,128)(2,1)S(1)} %collective-permute-done.10.x_ref), channel_id=1, source_target_pairs={{2,0},{3,1},{4,2},{5,3},{6,4},{7,5},{8,6},{9,7},{18,16},{19,17},{2... | collective-permute-start | bytes 2359304 | tf_op jit(solution)/shard_map/ppermute | solution.py:91
  65.4 3.9 %copy-start.11 = (bf16[192,2048]{1,0:T(8,128)(2,1)}, bf16[192,2048]{1,0:T(8,128)(2,1)S(1)}, u32[]{:S(2)}) copy-start(bf16[192,2048]{1,0:T(8,128)(2,1)S(1)} %collective-permute-done.6.x_ref) | copy-start | bytes 2359300
  65.4 23.2 %collective-permute-start.7 = (bf16[192,2048]{1,0:T(8,128)(2,1)S(1)}, bf16[192,2048]{1,0:T(8,128)(2,1)}, u32[]{:S(2)}, u32[]{:S(2)}) collective-permute-start(bf16[192,2048]{1,0:T(8,128)(2,1)S(1)} %collective-permute-done.6.x_ref), channel_id=1, source_target_pairs={{6,8},{7,9},{8,10},{9,11},{10,12},{11,13},{12,14},{13,15},{22,24},... | collective-permute-start | bytes 2359304 | tf_op jit(solution)/shard_map/ppermute | solution.py:91
  69.4 87.0 %all-to-all-start = ((bf16[8,192,256]{2,1,0:T(8,128)(2,1)}), bf16[8,192,256]{2,1,0:T(8,128)(2,1)S(1)}, u32[]{:S(2)}, u32[]{:S(2)}) async-start(bf16[8,192,256]{2,1,0:T(8,128)(2,1)} %bitcast.64), calls=%async_computation | async-start | bytes 1572864 | tf_op jit(solution)/shard_map/all_to_all | solution.py:94
  82.2 8.5 %copy-start.19 = (f32[1,2048,128]{2,1,0:T(8,128)S(1)}, f32[1,2048,128]{2,1,0:T(8,128)}, u32[]{:S(2)}) copy-start(f32[1,2048,128]{2,1,0:T(8,128)} %param.12) | copy-start | bytes 3145732
  88.7 66.4 %copy-start.2 = (bf16[192,2048]{1,0:T(8,128)(2,1)}, bf16[192,2048]{1,0:T(8,128)(2,1)S(1)}, u32[]{:S(2)}) copy-start(bf16[192,2048]{1,0:T(8,128)(2,1)S(1)} %broadcast_select_fusion.x_ref) | copy-start | bytes 2359300
  88.8 36.7 %collective-permute-start.12 = (bf16[192,2048]{1,0:T(8,128)(2,1)S(1)}, bf16[192,2048]{1,0:T(8,128)(2,1)S(1)}, u32[]{:S(2)}, u32[]{:S(2)}) collective-permute-start(bf16[192,2048]{1,0:T(8,128)(2,1)S(1)} %broadcast_select_fusion.x_ref), channel_id=1, source_target_pairs={{8,10},{9,11},{10,12},{11,13},{12,14},{13,15},{2,0},{3,1},{4,2},{5... | collective-permute-start | bytes 2359304 | tf_op jit(solution)/shard_map/ppermute | solution.py:119
  90.8 64.4 %collective-permute-start.15 = (bf16[2048,128]{1,0:T(8,128)(2,1)S(1)}, bf16[2048,128]{1,0:T(8,128)(2,1)}, u32[]{:S(2)}, u32[]{:S(2)}) collective-permute-start(bf16[2048,128]{1,0:T(8,128)(2,1)S(1)} %bitcast_convert_fusion), channel_id=1, source_target_pairs={{0,1},{1,0},{2,3},{3,2},{4,5},{5,4},{6,7},{7,6},{8,9},{9,8},{10,11... | collective-permute-start | bytes 1572872 | tf_op jit(solution)/shard_map/ppermute | solution.py:103
  125.5 27.3 %collective-permute-start.13 = (bf16[192,2048]{1,0:T(8,128)(2,1)S(1)}, bf16[192,2048]{1,0:T(8,128)(2,1)}, u32[]{:S(2)}, u32[]{:S(2)}) collective-permute-start(bf16[192,2048]{1,0:T(8,128)(2,1)S(1)} %collective-permute-done.12.x_ref), channel_id=1, source_target_pairs={{10,12},{11,13},{12,14},{13,15},{2,0},{3,1},{4,2},{5,3},{26,28},{2... | collective-permute-start | bytes 2359304 | tf_op jit(solution)/shard_map/ppermute | solution.py:119
  127.4 0.9 copy-start.17
  152.8 24.9 %collective-permute-start.14 = (bf16[192,2048]{1,0:T(8,128)(2,1)}, bf16[192,2048]{1,0:T(8,128)(2,1)}, u32[]{:S(2)}, u32[]{:S(2)}) collective-permute-start(bf16[192,2048]{1,0:T(8,128)(2,1)} %collective-permute-done.13.x_ref), channel_id=1, source_target_pairs={{12,14},{13,15},{2,0},{3,1},{28,30},{29,31},{18,16},{19,17},{44,46... | collective-permute-start | bytes 2359304 | tf_op jit(solution)/shard_map/ppermute | solution.py:119
  156.3 0.9 copy-start
  157.2 1.1 copy-start.4
  157.3 1.3 copy-start.1
  158.6 2.0 copy-start.16
  160.6 2.0 copy-start.10
  162.6 2.0 copy-start.14
  164.6 1.1 copy-start.8
  165.8 2.0 copy-start.12
  167.8 1.1 copy-start.6
  168.9 2.0 copy-start.3
  170.9 2.0 copy-start.18
  178.8 4.7 %collective-permute-start.16 = (f32[2048,128]{1,0:T(8,128)S(1)}, f32[2048,128]{1,0:T(8,128)}, u32[]{:S(2)}, u32[]{:S(2)}) collective-permute-start(f32[2048,128]{1,0:T(8,128)S(1)} %get-tuple-element.63), channel_id=1, source_target_pairs={{0,1},{1,0},{2,3},{3,2},{4,5},{5,4},{6,7},{7,6},{8,9},{9,8},{10,11... | collective-permute-start | bytes 3145736 | tf_op jit(solution)/shard_map/ppermute | solution.py:129
  186.5 17.2 %collective-permute-start.3 = (bf16[2048,128]{1,0:T(8,128)(2,1)S(1)}, bf16[2048,128]{1,0:T(8,128)(2,1)}, u32[]{:S(2)}, u32[]{:S(2)}) collective-permute-start(bf16[2048,128]{1,0:T(8,128)(2,1)S(1)} %param.3), channel_id=1, source_target_pairs={{0,128},{16,144},{32,160},{48,176},{64,192},{80,208},{96,224},{112... | collective-permute-start | bytes 1572872 | tf_op jit(solution)/shard_map/cond/branch_3_fun/ppermute | solution.py:75

commit v2 on v1

v2 whole, which is shorter than its diff:
```python
from functools import partial

import jax
import jax.numpy as jnp
from jax import lax
from jax.experimental import pallas as pl
from jax.experimental.pallas import tpu as pltpu
from jax.sharding import PartitionSpec as P

D_IN = 2048
HEAD = 128
CORES = 2
ROWS = 512
PARTS = 2
WAYS = (1, -1)
EXCHANGE = 5


def gradient_kernel(info, *refs):
    xs, (w_ref, cot_ref, own_in, other_in, own_out, other_out) = refs[:PARTS], refs[PARTS:]
    valid, source, core = info[0], info[1], info[2]

    @pl.when(valid > 0)
    def _():
        x = jnp.concatenate([ref[...] for ref in xs], axis=0)
        query = jnp.dot(x, w_ref[...], preferred_element_type=jnp.float32) * D_IN ** (-0.5)
        cot = cot_ref[source].astype(jnp.float32)
        first, second = cot[:, :HEAD], cot[:, HEAD:]
        upstreams = (
            jnp.where(core == 0, first, second),
            jnp.where(core == 0, second, first),
        )
        parts = []
        for at, upstream in enumerate(upstreams):
            shaped = query[:, at * HEAD : (at + 1) * HEAD]
            inverse = lax.rsqrt(jnp.mean(shaped * shaped, axis=-1, keepdims=True) + 1e-06)
            normed = shaped * inverse
            projected = jnp.mean(upstream * normed, axis=-1, keepdims=True)
            parts.append((inverse * (upstream - normed * projected)).astype(jnp.bfloat16))
        dquery = jnp.concatenate(parts, axis=1)
        for at in range(0, D_IN, ROWS):
            rows = slice(at, at + ROWS)
            part = lax.dot_general(
                jnp.concatenate([ref[:, rows] for ref in xs], axis=0),
                dquery,
                (((0,), (0,)), ((), ())),
                preferred_element_type=jnp.float32,
            )
            own_out[rows, :] = own_in[rows, :] + part[:, :HEAD]
            other_out[rows, :] = other_in[rows, :] + part[:, HEAD:]


def accumulate(sums, weights, cots, core, xs, valid, source):
    source = jnp.clip(source, 0, cots.shape[0] - 1)
    info = jnp.stack([jnp.int32(valid), source, core])
    vmem = pl.BlockSpec(memory_space=pltpu.VMEM)
    tokens = cots.shape[1]
    return pl.pallas_call(
        gradient_kernel,
        out_shape=[jax.ShapeDtypeStruct(s.shape, s.dtype) for s in sums],
        in_specs=[pl.BlockSpec(memory_space=pltpu.SMEM)] + [vmem] * (PARTS + 4),
        out_specs=[vmem, vmem],
        input_output_aliases={PARTS + 3: 0, PARTS + 4: 1},
        cost_estimate=pl.CostEstimate(
            flops=8 * tokens * D_IN * HEAD, bytes_accessed=6 * 2**20, transcendentals=2 * tokens
        ),
        compiler_params=pltpu.CompilerParams(vmem_limit_bytes=32 * 2**20),
    )(info, *xs, weights, cots, *sums)


def pull_fresh(value, distance):
    count = lax.axis_size("replica")
    pairs = [(source, (source + distance) % count) for source in range(count)]
    return lax.ppermute(value, "replica", pairs)


def body(features, cotangent, master, moment, variance, step_count):
    counter = step_count[0]
    selector = counter % 4
    params = master[0]
    tokens = features[0]
    devices = lax.axis_size("fsdp")
    chips = devices // CORES
    half = chips // 2
    index = lax.axis_index("fsdp")
    chip, core = index // CORES, index % CORES
    rows = tokens.shape[0]

    groups = [[at * CORES + c for at in range(chips)] for c in range(CORES)]
    swapped = [(at, at ^ 1) for at in range(devices)]
    mine = params.astype(jnp.bfloat16)
    weights = jnp.concatenate([mine, lax.ppermute(mine, "fsdp", swapped)], axis=1)
    cots = cotangent[0].reshape(rows, chips, CORES * HEAD).transpose(1, 0, 2)

    def pairs_of(step, ways):
        pairs = []
        for core_at, way in enumerate(ways):
            sources = range(step - 1, chips) if way > 0 else range(0, chips - step + 1)
            pairs += [
                (at * CORES + core_at, (at + way) * CORES + core_at)
                for at in sources
                if 0 <= at + way < chips
            ]
        return pairs

    def hop(parts, pairs):
        return [lax.ppermute(part, "fsdp", pairs) for part in parts]

    def exchange(cots, *parts):
        cots, *parts = lax.optimization_barrier((cots, *parts))
        cots = lax.all_to_all(
            cots, "fsdp", split_axis=0, concat_axis=0, axis_index_groups=groups
        )
        return cots, parts

    upper = chip >= half
    parts = jnp.split(tokens, PARTS, axis=0)
    waiting = [(parts, 1, chip)]
    one, two = list(parts), list(parts)
    for step in range(1, half + 1):
        if step == EXCHANGE:
            cots, (one[0], two[0]) = exchange(cots, one[0], two[0])
        one, two = hop(one, pairs_of(step, WAYS)), hop(two, pairs_of(step, [-way for way in WAYS]))
        lead = (core == 0) | (WAYS[0] == WAYS[1])
        if step < half:
            for xs, first in ((list(one), lead), (list(two), ~lead)):
                valid = jnp.where(first, chip >= step, chip < chips - step)
                waiting.append((xs, valid, jnp.where(first, chip - step, chip + step)))
    block = [jnp.where(upper == lead, a, b) for a, b in zip(one, two)]
    for step in range(half, chips):
        if step > half:
            if step == EXCHANGE:
                cots, (block[0],) = exchange(cots, block[0])
            both = sorted(set(pairs_of(step, (1, 1)) + pairs_of(step, (-1, -1))))
            block = hop(block, both)
        valid = jnp.where(upper, chip >= step, chip < chips - step)
        waiting.append((list(block), valid, jnp.where(upper, chip - step, chip + step)))
    sums = tuple(jnp.zeros((D_IN, HEAD), jnp.float32) for _ in range(2))
    for xs, valid, source in waiting:
        sums = accumulate(sums, weights, cots, core, xs, valid, source)
    own, other = sums
    summed = own + lax.ppermute(other, "fsdp", swapped)

    grads = summed * D_IN ** (-0.5)
    power = counter.astype(jnp.float32)
    correct_first = 1.0 - jnp.power(jnp.float32(0.9), power)
    correct_second = 1.0 - jnp.power(jnp.float32(0.999), power)
    first = 0.9 * moment[0].astype(jnp.float32) + 0.1 * grads
    second = 0.999 * variance[0] + 0.001 * grads * grads
    update = 0.1 * (
        first / correct_first / (jnp.sqrt(second / correct_second) + 1e-08) + 0.1 * params
    )
    fresh = params - update
    received = lax.switch(
        selector,
        [partial(pull_fresh, distance=1 << level) for level in range(4)],
        fresh.astype(jnp.bfloat16),
    )
    return (0.5 * (fresh + received.astype(jnp.float32)))[None]


def solution(mesh):
    placed = (
        P("replica", "fsdp", None),
        P("replica", "fsdp", None),
        P("replica", None, "fsdp"),
        P("replica", None, "fsdp"),
        P("replica", None, "fsdp"),
        P(),
    )
    return jax.shard_map(
        body, mesh=mesh, in_specs=placed, out_specs=P("replica", None, "fsdp"), check_vma=False
    )
```

time: 207 us -> 238 us (1.15)
  the two profiles are of different devices: /device:TPU:48 before, /device:TPU:65 now
where the time goes in v2:
time: 238 us; the launch traced here: 237 us
  waiting for transfers between devices  117 us (49%)
  starting transfers between devices  74.4 us (31%)
  Pallas kernels  18.9 us (8%)
  other arithmetic  14.1 us (6%)
  local copies, waits for them, and re-layouts  10.9 us (5%)
    ppermute x1, waiting for transfers between devices, pull_fresh(): return lax.ppermute(value, 'replica', pairs)  58.7 us
    ppermute x22, starting transfers between devices, hop(): return [lax.ppermute(part, 'fsdp', pairs) for part in parts]  56.6 us
    ppermute x22, waiting for transfers between devices, hop(): return [lax.ppermute(part, 'fsdp', pairs) for part in parts]  56.4 us
    pallas_call x11, Pallas kernels, accumulate(): pl.pallas_call(gradient_kernel, out_shape=[jax.ShapeDtypeStruct(s.shape,...  18.9 us
    all_to_all x1, starting transfers between devices, exchange(): lax.all_to_all(cots, 'fsdp', split_axis=0, concat_axis=0, axis_index_grou...  9.29 us
    unnamed x87, local copies, waits for them, and re-layouts  8.52 us
  transfers between devices with their start and end apart: 26, of which 11 were waited for; matrix products, arithmetic and copies ran while one was open for 5% of the time, Pallas kernels for 7%

profile of v2, /device:TPU:65, one launch (start us, length us, event | category | flops | bytes accessed | tf_op | source)
XLA Modules:
  0.0 236.7 jit_solution(18255114922268314620)
XLA Ops:
  1.2 3.5 %collective-permute-start.8 = (bf16[96,2048]{1,0:T(8,128)(2,1)S(1)}, bf16[96,2048]{1,0:T(8,128)(2,1)S(1)}, u32[]{:S(2)}, u32[]{:S(2)}) collective-permute-start(bf16[96,2048]{1,0:T(8,128)(2,1)S(1)} %get-tuple-element.71.refs_0_), channel_id=1, source_target_pairs={{2,0},{4,2},{6,4},{8,6},{10,8},{12,10},{14,12},{1,3},{3,5},{5,7},{... | collective-permute-start | bytes 1179656 | tf_op jit(solution)/shard_map/ppermute | solution.py:107
  4.7 1.9 collective-permute-start.4
  7.4 3.0 %collective-permute-done.8.refs_0_ = bf16[96,2048]{1,0:T(8,128)(2,1)S(1)} collective-permute-done((bf16[96,2048]{1,0:T(8,128)(2,1)S(1)}, bf16[96,2048]{1,0:T(8,128)(2,1)S(1)}, u32[]{:S(2)}, u32[]{:S(2)}) %collective-permute-start.8) | collective-permute-done | bytes 393248 | tf_op jit(solution)/shard_map/ppermute | solution.py:107
  10.4 4.7 %collective-permute-start.9 = (bf16[96,2048]{1,0:T(8,128)(2,1)S(1)}, bf16[96,2048]{1,0:T(8,128)(2,1)S(1)}, u32[]{:S(2)}, u32[]{:S(2)}) collective-permute-start(bf16[96,2048]{1,0:T(8,128)(2,1)S(1)} %collective-permute-done.8.refs_0_), channel_id=1, source_target_pairs={{2,0},{4,2},{6,4},{8,6},{10,8},{12,10},{3,5},{5,7},{7,9},{9,11},{1... | collective-permute-start | bytes 1179656 | tf_op jit(solution)/shard_map/ppermute | solution.py:107
  15.9 1.9 collective-permute-start.5
  18.6 1.9 collective-permute-start.15
  20.5 5.3 %collective-permute-start.19 = (bf16[96,2048]{1,0:T(8,128)(2,1)S(1)}, bf16[96,2048]{1,0:T(8,128)(2,1)S(1)}, u32[]{:S(2)}, u32[]{:S(2)}) collective-permute-start(bf16[96,2048]{1,0:T(8,128)(2,1)S(1)} %get-tuple-element.70.refs_1_), channel_id=1, source_target_pairs={{2,0},{4,2},{6,4},{8,6},{10,8},{12,10},{14,12},{1,3},{3,5},{5,7},{... | collective-permute-start | bytes 1179656 | tf_op jit(solution)/shard_map/ppermute | solution.py:107
  25.9 4.6 %collective-permute-start.10 = (bf16[96,2048]{1,0:T(8,128)(2,1)S(1)}, bf16[96,2048]{1,0:T(8,128)(2,1)S(1)}, u32[]{:S(2)}, u32[]{:S(2)}) collective-permute-start(bf16[96,2048]{1,0:T(8,128)(2,1)S(1)} %collective-permute-done.9.refs_0_), channel_id=1, source_target_pairs={{2,0},{4,2},{6,4},{8,6},{10,8},{5,7},{7,9},{9,11},{11,13},{13,15},... | collective-permute-start | bytes 1179656 | tf_op jit(solution)/shard_map/ppermute | solution.py:107
  31.2 1.9 collective-permute-start.6
  33.6 4.1 %collective-permute-start.16 = (bf16[96,2048]{1,0:T(8,128)(2,1)S(1)}, bf16[96,2048]{1,0:T(8,128)(2,1)S(1)}, u32[]{:S(2)}, u32[]{:S(2)}) collective-permute-start(bf16[96,2048]{1,0:T(8,128)(2,1)S(1)} %collective-permute-done.15.refs_1_), channel_id=1, source_target_pairs={{2,4},{4,6},{6,8},{8,10},{10,12},{12,14},{3,1},{5,3},{7,5},{9,7},{... | collective-permute-start | bytes 1179656 | tf_op jit(solution)/shard_map/ppermute | solution.py:107
  37.7 1.9 collective-permute-start.20
  39.7 3.3 %collective-permute-done.10.refs_0_ = bf16[96,2048]{1,0:T(8,128)(2,1)S(1)} collective-permute-done((bf16[96,2048]{1,0:T(8,128)(2,1)S(1)}, bf16[96,2048]{1,0:T(8,128)(2,1)S(1)}, u32[]{:S(2)}, u32[]{:S(2)}) %collective-permute-start.10) | collective-permute-done | bytes 393248 | tf_op jit(solution)/shard_map/ppermute | solution.py:107
  43.0 1.4 collective-permute-start.11
  44.4 1.9 collective-permute-start.7
  48.7 2.1 collective-permute-done.16.refs_1_
  50.9 3.8 %collective-permute-start.17 = (bf16[96,2048]{1,0:T(8,128)(2,1)S(1)}, bf16[96,2048]{1,0:T(8,128)(2,1)S(1)}, u32[]{:S(2)}, u32[]{:S(2)}) collective-permute-start(bf16[96,2048]{1,0:T(8,128)(2,1)S(1)} %collective-permute-done.16.refs_1_), channel_id=1, source_target_pairs={{4,6},{6,8},{8,10},{10,12},{12,14},{3,1},{5,3},{7,5},{9,7},{11,9},... | collective-permute-start | bytes 1179656 | tf_op jit(solution)/shard_map/ppermute | solution.py:107
  54.7 3.2 %collective-permute-start.21 = (bf16[96,2048]{1,0:T(8,128)(2,1)S(1)}, bf16[96,2048]{1,0:T(8,128)(2,1)S(1)}, u32[]{:S(2)}, u32[]{:S(2)}) collective-permute-start(bf16[96,2048]{1,0:T(8,128)(2,1)S(1)} %collective-permute-done.20.refs_1_), channel_id=1, source_target_pairs={{2,0},{4,2},{6,4},{8,6},{10,8},{5,7},{7,9},{9,11},{11,13},{13,15},... | collective-permute-start | bytes 1179656 | tf_op jit(solution)/shard_map/ppermute | solution.py:107
  57.9 2.3 collective-permute-done.7
  61.3 9.3 %all-to-all-start = ((bf16[8,192,256]{2,1,0:T(8,128)(2,1)}), bf16[8,192,256]{2,1,0:T(8,128)(2,1)S(1)}, u32[]{:S(2)}, u32[]{:S(2)}) async-start(bf16[8,192,256]{2,1,0:T(8,128)(2,1)} %bitcast.72), calls=%async_computation | async-start | bytes 1572864 | tf_op jit(solution)/shard_map/all_to_all | solution.py:111
  70.6 2.2 collective-permute-start.18
  72.8 1.4 collective-permute-start.22
  74.3 2.1 bitcast_convert_fusion
  76.4 2.2 collective-permute-start.26
  80.6 1.9 collective-permute-start.12
  82.5 30.0 %collective-permute-done.18 = bf16[96,2048]{1,0:T(8,128)(2,1)S(1)} collective-permute-done((bf16[96,2048]{1,0:T(8,128)(2,1)S(1)}, bf16[96,2048]{1,0:T(8,128)(2,1)S(1)}, u32[]{:S(2)}, u32[]{:S(2)}) %collective-permute-start.18) | collective-permute-done | bytes 393248 | tf_op jit(solution)/shard_map/ppermute | solution.py:107
  112.5 1.9 collective-permute-start.23
  117.2 3.6 %collective-permute-done.12.refs_0_ = bf16[96,2048]{1,0:T(8,128)(2,1)S(1)} collective-permute-done((bf16[96,2048]{1,0:T(8,128)(2,1)S(1)}, bf16[96,2048]{1,0:T(8,128)(2,1)S(1)}, u32[]{:S(2)}, u32[]{:S(2)}) %collective-permute-start.12) | collective-permute-done | bytes 393248 | tf_op jit(solution)/shard_map/ppermute | solution.py:107
  120.8 2.1 collective-permute-start.13
  123.6 5.6 %collective-permute-done.23.refs_1_ = bf16[96,2048]{1,0:T(8,128)(2,1)S(1)} collective-permute-done((bf16[96,2048]{1,0:T(8,128)(2,1)S(1)}, bf16[96,2048]{1,0:T(8,128)(2,1)S(1)}, u32[]{:S(2)}, u32[]{:S(2)}) %collective-permute-start.23) | collective-permute-done | bytes 393248 | tf_op jit(solution)/shard_map/ppermute | solution.py:107
  129.2 2.1 collective-permute-start.24
  132.1 1.4 collective-permute-start.14
  133.5 5.9 %collective-permute-done.24.refs_1_ = bf16[96,2048]{1,0:T(8,128)(2,1)} collective-permute-done((bf16[96,2048]{1,0:T(8,128)(2,1)S(1)}, bf16[96,2048]{1,0:T(8,128)(2,1)}, u32[]{:S(2)}, u32[]{:S(2)}) %collective-permute-start.24) | collective-permute-done | bytes 393248 | tf_op jit(solution)/shard_map/ppermute | solution.py:107
  139.5 1.4 collective-permute-start.25
  144.4 2.0 shard_map.64
  146.5 2.0 shard_map.65
  148.5 2.0 shard_map.66
  150.6 2.0 shard_map.67
  152.6 2.0 shard_map.68
  154.7 2.0 shard_map.69
  157.8 2.2 shard_map.71
  160.0 2.0 shard_map.72
  164.3 3.1 %collective-permute-start.27 = (f32[2048,128]{1,0:T(8,128)S(1)}, f32[2048,128]{1,0:T(8,128)}, u32[]{:S(2)}, u32[]{:S(2)}) collective-permute-start(f32[2048,128]{1,0:T(8,128)S(1)} %get-tuple-element.67), channel_id=1, source_target_pairs={{0,1},{1,0},{2,3},{3,2},{4,5},{5,4},{6,7},{7,6},{8,9},{9,8},{10,11... | collective-permute-start | bytes 3145736 | tf_op jit(solution)/shard_map/ppermute | solution.py:142
  168.1 1.6 collective-permute-done.27
  169.7 2.9 %fusion.6 = (bf16[2048,128]{1,0:T(8,128)(2,1)S(1)}, f32[2048,128]{1,0:T(8,128)S(1)}) fusion(f32[]{:T(128)S(6)} %sub.46, f32[1,2048,128]{2,1,0:T(8,128)} %param.14, f32[]{:T(128)S(6)} %sub.45, f32[2048,128]{1,0:T(8,128)S(1)} %get-tuple-element.66, f32[2048,128]{1,0:T(8,128)} %collective-permute-done.27, bf16[1,2048,128]{2,1,0:T(8,128)(2,1)} %param.13, ...), kind=kLoop, calls=%fused_computation.29 | loop fusion | flops 4980736 | bytes 6291464 | tf_op jit(solution)/shard_map/convert_element_type | solution.py:157
  172.7 61.9 %conditional.4 = (bf16[2048,128]{1,0:T(8,128)(2,1)}) conditional(s32[]{:T(128)} %clamp.3, bf16[2048,128]{1,0:T(8,128)(2,1)S(1)} %get-tuple-element.68, bf16[2048,128]{1,0:T(8,128)(2,1)S(1)} %get-tuple-element.68, bf16[2048,128]{1,0:T(8,128)(2,1)S(1)} %get-tuple-element.68, ...), branch_computations={%region_0.1_spmd, %region_1.2_spmd, %region_2.3_spmd, %region_3.4_... | conditional | bytes 2097200
  172.7 3.2 %collective-permute-start = (bf16[2048,128]{1,0:T(8,128)(2,1)S(1)}, bf16[2048,128]{1,0:T(8,128)(2,1)}, u32[]{:S(2)}, u32[]{:S(2)}) collective-permute-start(bf16[2048,128]{1,0:T(8,128)(2,1)S(1)} %param), channel_id=1, source_target_pairs={{0,16},{16,32},{32,48},{48,64},{64,80},{80,96},{96,112},{112,128},... | collective-permute-start | bytes 1572872 | tf_op jit(solution)/shard_map/cond/branch_0_fun/ppermute | solution.py:74
  175.9 58.7 %collective-permute-done = bf16[2048,128]{1,0:T(8,128)(2,1)} collective-permute-done((bf16[2048,128]{1,0:T(8,128)(2,1)S(1)}, bf16[2048,128]{1,0:T(8,128)(2,1)}, u32[]{:S(2)}, u32[]{:S(2)}) %collective-permute-start) | collective-permute-done | bytes 524320 | tf_op jit(solution)/shard_map/cond/branch_0_fun/ppermute | solution.py:74
  234.6 2.1 multiply_bitcast_fusion
  (124 shorter events, 21.2 us)
Async XLA Ops:
  1.2 9.2 %collective-permute-start.8 = (bf16[96,2048]{1,0:T(8,128)(2,1)S(1)}, bf16[96,2048]{1,0:T(8,128)(2,1)S(1)}, u32[]{:S(2)}, u32[]{:S(2)}) collective-permute-start(bf16[96,2048]{1,0:T(8,128)(2,1)S(1)} %get-tuple-element.71.refs_0_), channel_id=1, source_target_pairs={{2,0},{4,2},{6,4},{8,6},{10,8},{12,10},{14,12},{1,3},{3,5},{5,7},{... | collective-permute-start | bytes 1179656 | tf_op jit(solution)/shard_map/ppermute | solution.py:107
  4.7 11.2 %collective-permute-start.4 = (bf16[96,2048]{1,0:T(8,128)(2,1)S(1)}, bf16[96,2048]{1,0:T(8,128)(2,1)S(1)}, u32[]{:S(2)}, u32[]{:S(2)}) collective-permute-start(bf16[96,2048]{1,0:T(8,128)(2,1)S(1)} %get-tuple-element.71.refs_0_), channel_id=1, source_target_pairs={{0,2},{2,4},{4,6},{6,8},{8,10},{10,12},{12,14},{3,1},{5,3},{7,5},{... | collective-permute-start | bytes 1179656 | tf_op jit(solution)/shard_map/ppermute | solution.py:107
  10.4 15.4 %collective-permute-start.9 = (bf16[96,2048]{1,0:T(8,128)(2,1)S(1)}, bf16[96,2048]{1,0:T(8,128)(2,1)S(1)}, u32[]{:S(2)}, u32[]{:S(2)}) collective-permute-start(bf16[96,2048]{1,0:T(8,128)(2,1)S(1)} %collective-permute-done.8.refs_0_), channel_id=1, source_target_pairs={{2,0},{4,2},{6,4},{8,6},{10,8},{12,10},{3,5},{5,7},{7,9},{9,11},{1... | collective-permute-start | bytes 1179656 | tf_op jit(solution)/shard_map/ppermute | solution.py:107
  15.9 15.3 %collective-permute-start.5 = (bf16[96,2048]{1,0:T(8,128)(2,1)S(1)}, bf16[96,2048]{1,0:T(8,128)(2,1)S(1)}, u32[]{:S(2)}, u32[]{:S(2)}) collective-permute-start(bf16[96,2048]{1,0:T(8,128)(2,1)S(1)} %collective-permute-done.4.refs_0_), channel_id=1, source_target_pairs={{2,4},{4,6},{6,8},{8,10},{10,12},{12,14},{3,1},{5,3},{7,5},{9,7},{... | collective-permute-start | bytes 1179656 | tf_op jit(solution)/shard_map/ppermute | solution.py:107
  18.6 15.0 %collective-permute-start.15 = (bf16[96,2048]{1,0:T(8,128)(2,1)S(1)}, bf16[96,2048]{1,0:T(8,128)(2,1)S(1)}, u32[]{:S(2)}, u32[]{:S(2)}) collective-permute-start(bf16[96,2048]{1,0:T(8,128)(2,1)S(1)} %get-tuple-element.70.refs_1_), channel_id=1, source_target_pairs={{0,2},{2,4},{4,6},{6,8},{8,10},{10,12},{12,14},{3,1},{5,3},{7,5},{... | collective-permute-start | bytes 1179656 | tf_op jit(solution)/shard_map/ppermute | solution.py:107
  20.5 17.2 %collective-permute-start.19 = (bf16[96,2048]{1,0:T(8,128)(2,1)S(1)}, bf16[96,2048]{1,0:T(8,128)(2,1)S(1)}, u32[]{:S(2)}, u32[]{:S(2)}) collective-permute-start(bf16[96,2048]{1,0:T(8,128)(2,1)S(1)} %get-tuple-element.70.refs_1_), channel_id=1, source_target_pairs={{2,0},{4,2},{6,4},{8,6},{10,8},{12,10},{14,12},{1,3},{3,5},{5,7},{... | collective-permute-start | bytes 1179656 | tf_op jit(solution)/shard_map/ppermute | solution.py:107
  25.9 17.1 %collective-permute-start.10 = (bf16[96,2048]{1,0:T(8,128)(2,1)S(1)}, bf16[96,2048]{1,0:T(8,128)(2,1)S(1)}, u32[]{:S(2)}, u32[]{:S(2)}) collective-permute-start(bf16[96,2048]{1,0:T(8,128)(2,1)S(1)} %collective-permute-done.9.refs_0_), channel_id=1, source_target_pairs={{2,0},{4,2},{6,4},{8,6},{10,8},{5,7},{7,9},{9,11},{11,13},{13,15},... | collective-permute-start | bytes 1179656 | tf_op jit(solution)/shard_map/ppermute | solution.py:107
  31.2 17.5 %copy-start.14 = (bf16[96,2048]{1,0:T(8,128)(2,1)}, bf16[96,2048]{1,0:T(8,128)(2,1)S(1)}, u32[]{:S(2)}) copy-start(bf16[96,2048]{1,0:T(8,128)(2,1)S(1)} %collective-permute-done.5.refs_0_) | copy-start | bytes 1179652
  31.2 13.1 %collective-permute-start.6 = (bf16[96,2048]{1,0:T(8,128)(2,1)S(1)}, bf16[96,2048]{1,0:T(8,128)(2,1)S(1)}, u32[]{:S(2)}, u32[]{:S(2)}) collective-permute-start(bf16[96,2048]{1,0:T(8,128)(2,1)S(1)} %collective-permute-done.5.refs_0_), channel_id=1, source_target_pairs={{4,6},{6,8},{8,10},{10,12},{12,14},{3,1},{5,3},{7,5},{9,7},{11,9},... | collective-permute-start | bytes 1179656 | tf_op jit(solution)/shard_map/ppermute | solution.py:107
  33.6 15.1 %copy-start.22 = (bf16[96,2048]{1,0:T(8,128)(2,1)}, bf16[96,2048]{1,0:T(8,128)(2,1)S(1)}, u32[]{:S(2)}) copy-start(bf16[96,2048]{1,0:T(8,128)(2,1)S(1)} %collective-permute-done.15.refs_1_) | copy-start | bytes 1179652
  33.6 17.2 %collective-permute-start.16 = (bf16[96,2048]{1,0:T(8,128)(2,1)S(1)}, bf16[96,2048]{1,0:T(8,128)(2,1)S(1)}, u32[]{:S(2)}, u32[]{:S(2)}) collective-permute-start(bf16[96,2048]{1,0:T(8,128)(2,1)S(1)} %collective-permute-done.15.refs_1_), channel_id=1, source_target_pairs={{2,4},{4,6},{6,8},{8,10},{10,12},{12,14},{3,1},{5,3},{7,5},{9,7},{... | collective-permute-start | bytes 1179656 | tf_op jit(solution)/shard_map/ppermute | solution.py:107
  37.7 10.9 %copy-start.20 = (bf16[96,2048]{1,0:T(8,128)(2,1)}, bf16[96,2048]{1,0:T(8,128)(2,1)S(1)}, u32[]{:S(2)}) copy-start(bf16[96,2048]{1,0:T(8,128)(2,1)S(1)} %collective-permute-done.19.refs_1_) | copy-start | bytes 1179652
  37.7 16.9 %collective-permute-start.20 = (bf16[96,2048]{1,0:T(8,128)(2,1)S(1)}, bf16[96,2048]{1,0:T(8,128)(2,1)S(1)}, u32[]{:S(2)}, u32[]{:S(2)}) collective-permute-start(bf16[96,2048]{1,0:T(8,128)(2,1)S(1)} %collective-permute-done.19.refs_1_), channel_id=1, source_target_pairs={{2,0},{4,2},{6,4},{8,6},{10,8},{12,10},{3,5},{5,7},{7,9},{9,11},{1... | collective-permute-start | bytes 1179656 | tf_op jit(solution)/shard_map/ppermute | solution.py:107
  43.0 5.7 %copy-start.10 = (bf16[96,2048]{1,0:T(8,128)(2,1)}, bf16[96,2048]{1,0:T(8,128)(2,1)S(1)}, u32[]{:S(2)}) copy-start(bf16[96,2048]{1,0:T(8,128)(2,1)S(1)} %collective-permute-done.10.refs_0_) | copy-start | bytes 1179652
  43.0 15.0 %collective-permute-start.11 = (bf16[96,2048]{1,0:T(8,128)(2,1)S(1)}, bf16[96,2048]{1,0:T(8,128)(2,1)}, u32[]{:S(2)}, u32[]{:S(2)}) collective-permute-start(bf16[96,2048]{1,0:T(8,128)(2,1)S(1)} %collective-permute-done.10.refs_0_), channel_id=1, source_target_pairs={{2,0},{4,2},{6,4},{8,6},{7,9},{9,11},{11,13},{13,15},{18,16},{20,1... | collective-permute-start | bytes 1179656 | tf_op jit(solution)/shard_map/ppermute | solution.py:107
  44.4 4.3 %copy-start.18 = (bf16[96,2048]{1,0:T(8,128)(2,1)}, bf16[96,2048]{1,0:T(8,128)(2,1)S(1)}, u32[]{:S(2)}) copy-start(bf16[96,2048]{1,0:T(8,128)(2,1)S(1)} %collective-permute-done.6.refs_0_) | copy-start | bytes 1179652
  44.4 15.9 %collective-permute-start.7 = (bf16[96,2048]{1,0:T(8,128)(2,1)S(1)}, bf16[96,2048]{1,0:T(8,128)(2,1)}, u32[]{:S(2)}, u32[]{:S(2)}) collective-permute-start(bf16[96,2048]{1,0:T(8,128)(2,1)S(1)} %collective-permute-done.6.refs_0_), channel_id=1, source_target_pairs={{6,8},{8,10},{10,12},{12,14},{3,1},{5,3},{7,5},{9,7},{22,24},{24,2... | collective-permute-start | bytes 1179656 | tf_op jit(solution)/shard_map/ppermute | solution.py:107
  50.9 10.5 %copy-start.26 = (bf16[96,2048]{1,0:T(8,128)(2,1)}, bf16[96,2048]{1,0:T(8,128)(2,1)S(1)}, u32[]{:S(2)}) copy-start(bf16[96,2048]{1,0:T(8,128)(2,1)S(1)} %collective-permute-done.16.refs_1_) | copy-start | bytes 1179652
  50.9 19.8 %collective-permute-start.17 = (bf16[96,2048]{1,0:T(8,128)(2,1)S(1)}, bf16[96,2048]{1,0:T(8,128)(2,1)S(1)}, u32[]{:S(2)}, u32[]{:S(2)}) collective-permute-start(bf16[96,2048]{1,0:T(8,128)(2,1)S(1)} %collective-permute-done.16.refs_1_), channel_id=1, source_target_pairs={{4,6},{6,8},{8,10},{10,12},{12,14},{3,1},{5,3},{7,5},{9,7},{11,9},... | collective-permute-start | bytes 1179656 | tf_op jit(solution)/shard_map/ppermute | solution.py:107
  54.7 6.7 %copy-start.24 = (bf16[96,2048]{1,0:T(8,128)(2,1)}, bf16[96,2048]{1,0:T(8,128)(2,1)S(1)}, u32[]{:S(2)}) copy-start(bf16[96,2048]{1,0:T(8,128)(2,1)S(1)} %collective-permute-done.20.refs_1_) | copy-start | bytes 1179652
  54.7 18.2 %collective-permute-start.21 = (bf16[96,2048]{1,0:T(8,128)(2,1)S(1)}, bf16[96,2048]{1,0:T(8,128)(2,1)S(1)}, u32[]{:S(2)}, u32[]{:S(2)}) collective-permute-start(bf16[96,2048]{1,0:T(8,128)(2,1)S(1)} %collective-permute-done.20.refs_1_), channel_id=1, source_target_pairs={{2,0},{4,2},{6,4},{8,6},{10,8},{5,7},{7,9},{9,11},{11,13},{13,15},... | collective-permute-start | bytes 1179656 | tf_op jit(solution)/shard_map/ppermute | solution.py:107
  61.3 19.3 %copy-start.4 = (bf16[96,2048]{1,0:T(8,128)(2,1)}, bf16[96,2048]{1,0:T(8,128)(2,1)S(1)}, u32[]{:S(2)}) copy-start(bf16[96,2048]{1,0:T(8,128)(2,1)S(1)} %broadcast_select_fusion.1.refs_0_) | copy-start | bytes 1179652
  61.3 80.9 %all-to-all-start = ((bf16[8,192,256]{2,1,0:T(8,128)(2,1)}), bf16[8,192,256]{2,1,0:T(8,128)(2,1)S(1)}, u32[]{:S(2)}, u32[]{:S(2)}) async-start(bf16[8,192,256]{2,1,0:T(8,128)(2,1)} %bitcast.72), calls=%async_computation | async-start | bytes 1572864 | tf_op jit(solution)/shard_map/all_to_all | solution.py:111
  70.6 41.9 %copy-start.30 = (bf16[96,2048]{1,0:T(8,128)(2,1)}, bf16[96,2048]{1,0:T(8,128)(2,1)S(1)}, u32[]{:S(2)}) copy-start(bf16[96,2048]{1,0:T(8,128)(2,1)S(1)} %collective-permute-done.17.refs_1_) | copy-start | bytes 1179652
  70.6 41.8 %collective-permute-start.18 = (bf16[96,2048]{1,0:T(8,128)(2,1)S(1)}, bf16[96,2048]{1,0:T(8,128)(2,1)S(1)}, u32[]{:S(2)}, u32[]{:S(2)}) collective-permute-start(bf16[96,2048]{1,0:T(8,128)(2,1)S(1)} %collective-permute-done.17.refs_1_), channel_id=1, source_target_pairs={{6,8},{8,10},{10,12},{12,14},{3,1},{5,3},{7,5},{9,7},{22,24},{24,2... | collective-permute-start | bytes 1179656 | tf_op jit(solution)/shard_map/ppermute | solution.py:107
  72.8 39.7 %copy-start.28 = (bf16[96,2048]{1,0:T(8,128)(2,1)}, bf16[96,2048]{1,0:T(8,128)(2,1)S(1)}, u32[]{:S(2)}) copy-start(bf16[96,2048]{1,0:T(8,128)(2,1)S(1)} %collective-permute-done.21.refs_1_) | copy-start | bytes 1179652
  72.8 39.6 %collective-permute-start.22 = (bf16[96,2048]{1,0:T(8,128)(2,1)S(1)}, bf16[96,2048]{1,0:T(8,128)(2,1)}, u32[]{:S(2)}, u32[]{:S(2)}) collective-permute-start(bf16[96,2048]{1,0:T(8,128)(2,1)S(1)} %collective-permute-done.21.refs_1_), channel_id=1, source_target_pairs={{2,0},{4,2},{6,4},{8,6},{7,9},{9,11},{11,13},{13,15},{18,16},{20,1... | collective-permute-start | bytes 1179656 | tf_op jit(solution)/shard_map/ppermute | solution.py:107
  76.4 64.5 %collective-permute-start.26 = (bf16[2048,128]{1,0:T(8,128)(2,1)}, bf16[2048,128]{1,0:T(8,128)(2,1)}, u32[]{:S(2)}, u32[]{:S(2)}) collective-permute-start(bf16[2048,128]{1,0:T(8,128)(2,1)} %bitcast_convert_fusion), channel_id=1, source_target_pairs={{0,1},{1,0},{2,3},{3,2},{4,5},{5,4},{6,7},{7,6},{8,9},{9,8},{10,11... | collective-permute-start | bytes 1572872 | tf_op jit(solution)/shard_map/ppermute | solution.py:92
  80.6 40.2 %collective-permute-start.12 = (bf16[96,2048]{1,0:T(8,128)(2,1)S(1)}, bf16[96,2048]{1,0:T(8,128)(2,1)S(1)}, u32[]{:S(2)}, u32[]{:S(2)}) collective-permute-start(bf16[96,2048]{1,0:T(8,128)(2,1)S(1)} %broadcast_select_fusion.1.refs_0_), channel_id=1, source_target_pairs={{2,0},{3,1},{4,2},{5,3},{6,4},{7,5},{8,10},{9,11},{10,12},{11,13},... | collective-permute-start | bytes 1179656 | tf_op jit(solution)/shard_map/ppermute | solution.py:107
  112.5 16.7 %collective-permute-start.23 = (bf16[96,2048]{1,0:T(8,128)(2,1)S(1)}, bf16[96,2048]{1,0:T(8,128)(2,1)S(1)}, u32[]{:S(2)}, u32[]{:S(2)}) collective-permute-start(bf16[96,2048]{1,0:T(8,128)(2,1)S(1)} %broadcast_select_fusion.refs_1_), channel_id=1, source_target_pairs={{2,0},{3,1},{4,2},{5,3},{6,4},{7,5},{8,10},{9,11},{10,12},{11,13},... | collective-permute-start | bytes 1179656 | tf_op jit(solution)/shard_map/ppermute | solution.py:107
  120.8 11.3 %collective-permute-start.13 = (bf16[96,2048]{1,0:T(8,128)(2,1)S(1)}, bf16[96,2048]{1,0:T(8,128)(2,1)}, u32[]{:S(2)}, u32[]{:S(2)}) collective-permute-start(bf16[96,2048]{1,0:T(8,128)(2,1)S(1)} %collective-permute-done.12.refs_0_), channel_id=1, source_target_pairs={{2,0},{3,1},{4,2},{5,3},{10,12},{11,13},{12,14},{13,15},{18,16},{1... | collective-permute-start | bytes 1179656 | tf_op jit(solution)/shard_map/ppermute | solution.py:107
  129.2 13.0 %copy-start.34 = (bf16[96,2048]{1,0:T(8,128)(2,1)}, bf16[96,2048]{1,0:T(8,128)(2,1)S(1)}, u32[]{:S(2)}) copy-start(bf16[96,2048]{1,0:T(8,128)(2,1)S(1)} %collective-permute-done.23.refs_1_) | copy-start | bytes 1179652
  129.2 10.3 %collective-permute-start.24 = (bf16[96,2048]{1,0:T(8,128)(2,1)S(1)}, bf16[96,2048]{1,0:T(8,128)(2,1)}, u32[]{:S(2)}, u32[]{:S(2)}) collective-permute-start(bf16[96,2048]{1,0:T(8,128)(2,1)S(1)} %collective-permute-done.23.refs_1_), channel_id=1, source_target_pairs={{2,0},{3,1},{4,2},{5,3},{10,12},{11,13},{12,14},{13,15},{18,16},{1... | collective-permute-start | bytes 1179656 | tf_op jit(solution)/shard_map/ppermute | solution.py:107
  132.1 31.0 %collective-permute-start.14 = (bf16[96,2048]{1,0:T(8,128)(2,1)}, bf16[96,2048]{1,0:T(8,128)(2,1)}, u32[]{:S(2)}, u32[]{:S(2)}) collective-permute-start(bf16[96,2048]{1,0:T(8,128)(2,1)} %collective-permute-done.13.refs_0_), channel_id=1, source_target_pairs={{2,0},{3,1},{12,14},{13,15},{18,16},{19,17},{28,30},{29,31},{34,32... | collective-permute-start | bytes 1179656 | tf_op jit(solution)/shard_map/ppermute | solution.py:107
  139.5 23.6 %collective-permute-start.25 = (bf16[96,2048]{1,0:T(8,128)(2,1)}, bf16[96,2048]{1,0:T(8,128)(2,1)}, u32[]{:S(2)}, u32[]{:S(2)}) collective-permute-start(bf16[96,2048]{1,0:T(8,128)(2,1)} %collective-permute-done.24.refs_1_), channel_id=1, source_target_pairs={{2,0},{3,1},{12,14},{13,15},{18,16},{19,17},{28,30},{29,31},{34,32... | collective-permute-start | bytes 1179656 | tf_op jit(solution)/shard_map/ppermute | solution.py:107
  146.4 2.0 copy-start.13
  146.4 2.0 copy-start.21
  146.4 2.0 copy-start.36
  148.5 2.0 copy-start.15
  148.5 2.0 copy-start.27
  148.5 2.0 copy-start.42
  150.5 2.0 copy-start.9
  150.5 2.0 copy-start.25
  150.5 2.0 copy-start.40
  157.8 2.2 copy-start.33
  157.8 2.2 copy-start.35
  164.3 5.5 %collective-permute-start.27 = (f32[2048,128]{1,0:T(8,128)S(1)}, f32[2048,128]{1,0:T(8,128)}, u32[]{:S(2)}, u32[]{:S(2)}) collective-permute-start(f32[2048,128]{1,0:T(8,128)S(1)} %get-tuple-element.67), channel_id=1, source_target_pairs={{0,1},{1,0},{2,3},{3,2},{4,5},{5,4},{6,7},{7,6},{8,9},{9,8},{10,11... | collective-permute-start | bytes 3145736 | tf_op jit(solution)/shard_map/ppermute | solution.py:142
  172.7 61.9 %collective-permute-start = (bf16[2048,128]{1,0:T(8,128)(2,1)S(1)}, bf16[2048,128]{1,0:T(8,128)(2,1)}, u32[]{:S(2)}, u32[]{:S(2)}) collective-permute-start(bf16[2048,128]{1,0:T(8,128)(2,1)S(1)} %param), channel_id=1, source_target_pairs={{0,16},{16,32},{32,48},{48,64},{64,80},{80,96},{96,112},{112,128},... | collective-permute-start | bytes 1572872 | tf_op jit(solution)/shard_map/cond/branch_0_fun/ppermute | solution.py:74
  (21 other events, 28.0 us)

commit v3 on v2

--- a/solution.py
+++ b/solution.py
@@ -10,6 +10,7 @@
 D_IN = 2048
 HEAD = 128
 CORES = 2
+LINES = 4
 ROWS = 512
 PARTS = 2
 WAYS = (1, -1)
@@ -70,8 +71,36 @@
 
 def pull_fresh(value, distance):
     count = lax.axis_size("replica")
-    pairs = [(source, (source + distance) % count) for source in range(count)]
-    return lax.ppermute(value, "replica", pairs)
+    if distance >= LINES:
+        pairs = [(source, (source + distance) % count) for source in range(count)]
+        return lax.ppermute(value, "replica", pairs)
+
+    groups = range(0, count, LINES)
+    line = lax.axis_index("replica") % LINES
+    leaving = range(LINES - distance, LINES)
+    lanes = LINES // distance
+    slices = jnp.split(value, lanes)
+    near = [(g + y, g + y + distance) for g in groups for y in range(LINES - distance)]
+    held = []
+    for k, part in enumerate(slices[:-1]):
+        held.append(
+            lax.ppermute(
+                part,
+                "replica",
+                [(g + y, g + (y + distance * (k + 1)) % LINES) for g in groups for y in leaving],
+            )
+        )
+    held.append(slices[-1])
+    direct = lax.ppermute(value, "replica", near)
+    far = []
+    for k, part in enumerate(held):
+        way = [
+            (g + (y + distance * (k + 1)) % LINES, (g + y + distance) % count)
+            for g in groups
+            for y in leaving
+        ]
+        far.append(lax.ppermute(part, "replica", way))
+    return jnp.where(line < distance, jnp.concatenate(far), direct)
 
 
 def body(features, cotangent, master, moment, variance, step_count):

time: 238 us -> 238 us (level)
  the two profiles are of different devices: /device:TPU:65 before, /device:TPU:73 now
where the time goes in v3:
time: 238 us; the launch traced here: 237 us
  waiting for transfers between devices  102 us (43%)
  starting transfers between devices  88.5 us (37%)
  Pallas kernels  18.9 us (8%)
  other arithmetic  14 us (6%)
  local copies, waits for them, and re-layouts  11.6 us (5%)
    ppermute x22, starting transfers between devices, hop(): return [lax.ppermute(part, 'fsdp', pairs) for part in parts]  57.2 us
    ppermute x22, waiting for transfers between devices, hop(): return [lax.ppermute(part, 'fsdp', pairs) for part in parts]  50.6 us
    ppermute x1, waiting for transfers between devices, pull_fresh(): return lax.ppermute(value, 'replica', pairs)  49.5 us
    pallas_call x11, Pallas kernels, accumulate(): pl.pallas_call(gradient_kernel, out_shape=[jax.ShapeDtypeStruct(s.shape,...  18.9 us
    all_to_all x1, starting transfers between devices, exchange(): lax.all_to_all(cots, 'fsdp', split_axis=0, concat_axis=0, axis_index_grou...  12.8 us
    unnamed x87, local copies, waits for them, and re-layouts  9.29 us
    ppermute x1, starting transfers between devices, pull_fresh(): return lax.ppermute(value, 'replica', pairs)  8.57 us
    ppermute x1, starting transfers between devices, body(): summed = own + lax.ppermute(other, 'fsdp', swapped)  5.12 us
  transfers between devices with their start and end apart: 26, of which 10 were waited for; matrix products, arithmetic and copies ran while one was open for 5% of the time, Pallas kernels for 7%

profile of v3, /device:TPU:73, one launch (start us, length us, event | category | flops | bytes accessed | tf_op | source)
XLA Modules:
  0.0 236.5 jit_solution(1190963364479881152)
XLA Ops:
  1.2 1.9 collective-permute-start.14
  3.1 3.5 %collective-permute-start.18 = (bf16[96,2048]{1,0:T(8,128)(2,1)S(1)}, bf16[96,2048]{1,0:T(8,128)(2,1)S(1)}, u32[]{:S(2)}, u32[]{:S(2)}) collective-permute-start(bf16[96,2048]{1,0:T(8,128)(2,1)S(1)} %get-tuple-element.77.refs_0_), channel_id=1, source_target_pairs={{2,0},{4,2},{6,4},{8,6},{10,8},{12,10},{14,12},{1,3},{3,5},{5,7},{... | collective-permute-start | bytes 1179656 | tf_op jit(solution)/shard_map/ppermute | solution.py:136
  7.4 2.7 %collective-permute-done.14.refs_0_ = bf16[96,2048]{1,0:T(8,128)(2,1)S(1)} collective-permute-done((bf16[96,2048]{1,0:T(8,128)(2,1)S(1)}, bf16[96,2048]{1,0:T(8,128)(2,1)S(1)}, u32[]{:S(2)}, u32[]{:S(2)}) %collective-permute-start.14) | collective-permute-done | bytes 393248 | tf_op jit(solution)/shard_map/ppermute | solution.py:136
  10.2 1.9 collective-permute-start.15
  12.8 2.5 %collective-permute-done.18.refs_0_ = bf16[96,2048]{1,0:T(8,128)(2,1)S(1)} collective-permute-done((bf16[96,2048]{1,0:T(8,128)(2,1)S(1)}, bf16[96,2048]{1,0:T(8,128)(2,1)S(1)}, u32[]{:S(2)}, u32[]{:S(2)}) %collective-permute-start.18) | collective-permute-done | bytes 393248 | tf_op jit(solution)/shard_map/ppermute | solution.py:136
  15.3 4.2 %collective-permute-start.19 = (bf16[96,2048]{1,0:T(8,128)(2,1)S(1)}, bf16[96,2048]{1,0:T(8,128)(2,1)S(1)}, u32[]{:S(2)}, u32[]{:S(2)}) collective-permute-start(bf16[96,2048]{1,0:T(8,128)(2,1)S(1)} %collective-permute-done.18.refs_0_), channel_id=1, source_target_pairs={{2,0},{4,2},{6,4},{8,6},{10,8},{12,10},{3,5},{5,7},{7,9},{9,11},{1... | collective-permute-start | bytes 1179656 | tf_op jit(solution)/shard_map/ppermute | solution.py:136
  20.3 1.9 collective-permute-start.25
  22.2 5.0 %collective-permute-start.29 = (bf16[96,2048]{1,0:T(8,128)(2,1)S(1)}, bf16[96,2048]{1,0:T(8,128)(2,1)S(1)}, u32[]{:S(2)}, u32[]{:S(2)}) collective-permute-start(bf16[96,2048]{1,0:T(8,128)(2,1)S(1)} %get-tuple-element.76.refs_1_), channel_id=1, source_target_pairs={{2,0},{4,2},{6,4},{8,6},{10,8},{12,10},{14,12},{1,3},{3,5},{5,7},{... | collective-permute-start | bytes 1179656 | tf_op jit(solution)/shard_map/ppermute | solution.py:136
  27.2 1.9 collective-permute-start.16
  29.9 4.6 %collective-permute-start.20 = (bf16[96,2048]{1,0:T(8,128)(2,1)S(1)}, bf16[96,2048]{1,0:T(8,128)(2,1)S(1)}, u32[]{:S(2)}, u32[]{:S(2)}) collective-permute-start(bf16[96,2048]{1,0:T(8,128)(2,1)S(1)} %collective-permute-done.19.refs_0_), channel_id=1, source_target_pairs={{2,0},{4,2},{6,4},{8,6},{10,8},{5,7},{7,9},{9,11},{11,13},{13,15},... | collective-permute-start | bytes 1179656 | tf_op jit(solution)/shard_map/ppermute | solution.py:136
  35.3 1.9 collective-permute-start.26
  37.2 4.6 %collective-permute-start.30 = (bf16[96,2048]{1,0:T(8,128)(2,1)S(1)}, bf16[96,2048]{1,0:T(8,128)(2,1)S(1)}, u32[]{:S(2)}, u32[]{:S(2)}) collective-permute-start(bf16[96,2048]{1,0:T(8,128)(2,1)S(1)} %collective-permute-done.29.refs_1_), channel_id=1, source_target_pairs={{2,0},{4,2},{6,4},{8,6},{10,8},{12,10},{3,5},{5,7},{7,9},{9,11},{1... | collective-permute-start | bytes 1179656 | tf_op jit(solution)/shard_map/ppermute | solution.py:136
  43.1 1.9 collective-permute-start.17
  45.0 1.5 collective-permute-start.21
  46.5 1.3 copy.30
  48.9 2.6 %collective-permute-done.26.refs_1_ = bf16[96,2048]{1,0:T(8,128)(2,1)S(1)} collective-permute-done((bf16[96,2048]{1,0:T(8,128)(2,1)S(1)}, bf16[96,2048]{1,0:T(8,128)(2,1)S(1)}, u32[]{:S(2)}, u32[]{:S(2)}) %collective-permute-start.26) | collective-permute-done | bytes 393248 | tf_op jit(solution)/shard_map/ppermute | solution.py:136
  51.5 1.9 collective-permute-start.27
  53.5 6.8 %collective-permute-start.31 = (bf16[96,2048]{1,0:T(8,128)(2,1)S(1)}, bf16[96,2048]{1,0:T(8,128)(2,1)S(1)}, u32[]{:S(2)}, u32[]{:S(2)}) collective-permute-start(bf16[96,2048]{1,0:T(8,128)(2,1)S(1)} %collective-permute-done.30.refs_1_), channel_id=1, source_target_pairs={{2,0},{4,2},{6,4},{8,6},{10,8},{5,7},{7,9},{9,11},{11,13},{13,15},... | collective-permute-start | bytes 1179656 | tf_op jit(solution)/shard_map/ppermute | solution.py:136
  61.3 12.8 %all-to-all-start = ((bf16[8,192,256]{2,1,0:T(8,128)(2,1)}), bf16[8,192,256]{2,1,0:T(8,128)(2,1)S(1)}, u32[]{:S(2)}, u32[]{:S(2)}) async-start(bf16[8,192,256]{2,1,0:T(8,128)(2,1)} %bitcast.72), calls=%async_computation | async-start | bytes 1572864 | tf_op jit(solution)/shard_map/all_to_all | solution.py:140
  74.1 2.2 collective-permute-start.28
  77.1 2.1 bitcast_convert_fusion
  79.1 4.9 %collective-permute-start.36 = (bf16[2048,128]{1,0:T(8,128)(2,1)}, bf16[2048,128]{1,0:T(8,128)(2,1)}, u32[]{:S(2)}, u32[]{:S(2)}) collective-permute-start(bf16[2048,128]{1,0:T(8,128)(2,1)} %bitcast_convert_fusion), channel_id=1, source_target_pairs={{0,1},{1,0},{2,3},{3,2},{4,5},{5,4},{6,7},{7,6},{8,9},{9,8},{10,11... | collective-permute-start | bytes 1572872 | tf_op jit(solution)/shard_map/ppermute | solution.py:121
  86.0 1.9 collective-permute-start.22
  87.9 25.1 %collective-permute-done.28 = bf16[96,2048]{1,0:T(8,128)(2,1)S(1)} collective-permute-done((bf16[96,2048]{1,0:T(8,128)(2,1)S(1)}, bf16[96,2048]{1,0:T(8,128)(2,1)S(1)}, u32[]{:S(2)}, u32[]{:S(2)}) %collective-permute-start.28) | collective-permute-done | bytes 393248 | tf_op jit(solution)/shard_map/ppermute | solution.py:136
  113.1 1.9 collective-permute-start.33
  117.7 4.7 %collective-permute-done.22.refs_0_ = bf16[96,2048]{1,0:T(8,128)(2,1)S(1)} collective-permute-done((bf16[96,2048]{1,0:T(8,128)(2,1)S(1)}, bf16[96,2048]{1,0:T(8,128)(2,1)S(1)}, u32[]{:S(2)}, u32[]{:S(2)}) %collective-permute-start.22) | collective-permute-done | bytes 393248 | tf_op jit(solution)/shard_map/ppermute | solution.py:136
  122.4 2.1 collective-permute-start.23
  124.4 6.3 %collective-permute-done.33.refs_1_ = bf16[96,2048]{1,0:T(8,128)(2,1)S(1)} collective-permute-done((bf16[96,2048]{1,0:T(8,128)(2,1)S(1)}, bf16[96,2048]{1,0:T(8,128)(2,1)S(1)}, u32[]{:S(2)}, u32[]{:S(2)}) %collective-permute-start.33) | collective-permute-done | bytes 393248 | tf_op jit(solution)/shard_map/ppermute | solution.py:136
  130.8 2.1 collective-permute-start.34
  134.4 1.4 collective-permute-start.24
  135.8 5.2 %collective-permute-done.34.refs_1_ = bf16[96,2048]{1,0:T(8,128)(2,1)} collective-permute-done((bf16[96,2048]{1,0:T(8,128)(2,1)S(1)}, bf16[96,2048]{1,0:T(8,128)(2,1)}, u32[]{:S(2)}, u32[]{:S(2)}) %collective-permute-start.34) | collective-permute-done | bytes 393248 | tf_op jit(solution)/shard_map/ppermute | solution.py:136
  141.1 1.4 collective-permute-start.35
  142.5 1.3 pad_maximum_fusion.refs_2_
  146.0 2.0 shard_map.64
  148.0 2.0 shard_map.65
  150.1 2.0 shard_map.66
  152.1 2.0 shard_map.67
  154.2 2.0 shard_map.68
  156.2 2.0 shard_map.69
  159.4 2.2 shard_map.71
  161.6 2.0 shard_map.72
  165.9 5.1 %collective-permute-start.37 = (f32[2048,128]{1,0:T(8,128)S(1)}, f32[2048,128]{1,0:T(8,128)}, u32[]{:S(2)}, u32[]{:S(2)}) collective-permute-start(f32[2048,128]{1,0:T(8,128)S(1)} %get-tuple-element.67), channel_id=1, source_target_pairs={{0,1},{1,0},{2,3},{3,2},{4,5},{5,4},{6,7},{7,6},{8,9},{9,8},{10,11... | collective-permute-start | bytes 3145736 | tf_op jit(solution)/shard_map/ppermute | solution.py:171
  171.7 1.6 collective-permute-done.37
  173.4 2.9 %fusion.6 = (bf16[2048,128]{1,0:T(8,128)(2,1)S(1)}, f32[2048,128]{1,0:T(8,128)S(1)}) fusion(f32[]{:T(128)S(6)} %sub.46, f32[1,2048,128]{2,1,0:T(8,128)} %param.14, f32[]{:T(128)S(6)} %sub.45, f32[2048,128]{1,0:T(8,128)S(1)} %get-tuple-element.66, f32[2048,128]{1,0:T(8,128)} %collective-permute-done.37, bf16[1,2048,128]{2,1,0:T(8,128)(2,1)} %param.13, ...), kind=kLoop, calls=%fused_computation.31 | loop fusion | flops 4980736 | bytes 6291464 | tf_op jit(solution)/shard_map/convert_element_type | solution.py:186
  176.3 58.1 %conditional.4 = (bf16[2048,128]{1,0:T(8,128)(2,1)}) conditional(s32[]{:T(128)} %clamp.3, bf16[2048,128]{1,0:T(8,128)(2,1)S(1)} %get-tuple-element.68, bf16[2048,128]{1,0:T(8,128)(2,1)S(1)} %get-tuple-element.68, bf16[2048,128]{1,0:T(8,128)(2,1)S(1)} %get-tuple-element.68, ...), branch_computations={%region_0.1_spmd, %region_1.2_spmd, %region_2.3_spmd, %region_3.4_... | conditional | flops 2359311 | bytes 8389087
  176.3 8.6 %collective-permute-start = (bf16[2048,128]{1,0:T(8,128)(2,1)S(1)}, bf16[2048,128]{1,0:T(8,128)(2,1)}, u32[]{:S(2)}, u32[]{:S(2)}) collective-permute-start(bf16[2048,128]{1,0:T(8,128)(2,1)S(1)} %param.2), channel_id=1, source_target_pairs={{0,64},{16,80},{32,96},{48,112},{64,128},{80,144},{96,160},{112,17... | collective-permute-start | bytes 1572872 | tf_op jit(solution)/shard_map/cond/branch_2_fun/ppermute | solution.py:76
  184.9 49.5 %collective-permute-done = bf16[2048,128]{1,0:T(8,128)(2,1)} collective-permute-done((bf16[2048,128]{1,0:T(8,128)(2,1)S(1)}, bf16[2048,128]{1,0:T(8,128)(2,1)}, u32[]{:S(2)}, u32[]{:S(2)}) %collective-permute-start) | collective-permute-done | bytes 524320 | tf_op jit(solution)/shard_map/cond/branch_2_fun/ppermute | solution.py:76
  234.4 2.1 multiply_bitcast_fusion
  (124 shorter events, 20.7 us)
Async XLA Ops:
  1.2 9.0 %collective-permute-start.14 = (bf16[96,2048]{1,0:T(8,128)(2,1)S(1)}, bf16[96,2048]{1,0:T(8,128)(2,1)S(1)}, u32[]{:S(2)}, u32[]{:S(2)}) collective-permute-start(bf16[96,2048]{1,0:T(8,128)(2,1)S(1)} %get-tuple-element.77.refs_0_), channel_id=1, source_target_pairs={{0,2},{2,4},{4,6},{6,8},{8,10},{10,12},{12,14},{3,1},{5,3},{7,5},{... | collective-permute-start | bytes 1179656 | tf_op jit(solution)/shard_map/ppermute | solution.py:136
  3.1 12.2 %collective-permute-start.18 = (bf16[96,2048]{1,0:T(8,128)(2,1)S(1)}, bf16[96,2048]{1,0:T(8,128)(2,1)S(1)}, u32[]{:S(2)}, u32[]{:S(2)}) collective-permute-start(bf16[96,2048]{1,0:T(8,128)(2,1)S(1)} %get-tuple-element.77.refs_0_), channel_id=1, source_target_pairs={{2,0},{4,2},{6,4},{8,6},{10,8},{12,10},{14,12},{1,3},{3,5},{5,7},{... | collective-permute-start | bytes 1179656 | tf_op jit(solution)/shard_map/ppermute | solution.py:136
  10.2 17.1 %collective-permute-start.15 = (bf16[96,2048]{1,0:T(8,128)(2,1)S(1)}, bf16[96,2048]{1,0:T(8,128)(2,1)S(1)}, u32[]{:S(2)}, u32[]{:S(2)}) collective-permute-start(bf16[96,2048]{1,0:T(8,128)(2,1)S(1)} %collective-permute-done.14.refs_0_), channel_id=1, source_target_pairs={{2,4},{4,6},{6,8},{8,10},{10,12},{12,14},{3,1},{5,3},{7,5},{9,7},{... | collective-permute-start | bytes 1179656 | tf_op jit(solution)/shard_map/ppermute | solution.py:136
  15.3 14.6 %collective-permute-start.19 = (bf16[96,2048]{1,0:T(8,128)(2,1)S(1)}, bf16[96,2048]{1,0:T(8,128)(2,1)S(1)}, u32[]{:S(2)}, u32[]{:S(2)}) collective-permute-start(bf16[96,2048]{1,0:T(8,128)(2,1)S(1)} %collective-permute-done.18.refs_0_), channel_id=1, source_target_pairs={{2,0},{4,2},{6,4},{8,6},{10,8},{12,10},{3,5},{5,7},{7,9},{9,11},{1... | collective-permute-start | bytes 1179656 | tf_op jit(solution)/shard_map/ppermute | solution.py:136
  20.3 15.0 %collective-permute-start.25 = (bf16[96,2048]{1,0:T(8,128)(2,1)S(1)}, bf16[96,2048]{1,0:T(8,128)(2,1)S(1)}, u32[]{:S(2)}, u32[]{:S(2)}) collective-permute-start(bf16[96,2048]{1,0:T(8,128)(2,1)S(1)} %get-tuple-element.76.refs_1_), channel_id=1, source_target_pairs={{0,2},{2,4},{4,6},{6,8},{8,10},{10,12},{12,14},{3,1},{5,3},{7,5},{... | collective-permute-start | bytes 1179656 | tf_op jit(solution)/shard_map/ppermute | solution.py:136
  22.2 15.0 %collective-permute-start.29 = (bf16[96,2048]{1,0:T(8,128)(2,1)S(1)}, bf16[96,2048]{1,0:T(8,128)(2,1)S(1)}, u32[]{:S(2)}, u32[]{:S(2)}) collective-permute-start(bf16[96,2048]{1,0:T(8,128)(2,1)S(1)} %get-tuple-element.76.refs_1_), channel_id=1, source_target_pairs={{2,0},{4,2},{6,4},{8,6},{10,8},{12,10},{14,12},{1,3},{3,5},{5,7},{... | collective-permute-start | bytes 1179656 | tf_op jit(solution)/shard_map/ppermute | solution.py:136
  27.2 15.8 %collective-permute-start.16 = (bf16[96,2048]{1,0:T(8,128)(2,1)S(1)}, bf16[96,2048]{1,0:T(8,128)(2,1)S(1)}, u32[]{:S(2)}, u32[]{:S(2)}) collective-permute-start(bf16[96,2048]{1,0:T(8,128)(2,1)S(1)} %collective-permute-done.15.refs_0_), channel_id=1, source_target_pairs={{4,6},{6,8},{8,10},{10,12},{12,14},{3,1},{5,3},{7,5},{9,7},{11,9},... | collective-permute-start | bytes 1179656 | tf_op jit(solution)/shard_map/ppermute | solution.py:136
  29.9 15.1 %collective-permute-start.20 = (bf16[96,2048]{1,0:T(8,128)(2,1)S(1)}, bf16[96,2048]{1,0:T(8,128)(2,1)S(1)}, u32[]{:S(2)}, u32[]{:S(2)}) collective-permute-start(bf16[96,2048]{1,0:T(8,128)(2,1)S(1)} %collective-permute-done.19.refs_0_), channel_id=1, source_target_pairs={{2,0},{4,2},{6,4},{8,6},{10,8},{5,7},{7,9},{9,11},{11,13},{13,15},... | collective-permute-start | bytes 1179656 | tf_op jit(solution)/shard_map/ppermute | solution.py:136
  35.3 13.6 %copy-start.22 = (bf16[96,2048]{1,0:T(8,128)(2,1)}, bf16[96,2048]{1,0:T(8,128)(2,1)S(1)}, u32[]{:S(2)}) copy-start(bf16[96,2048]{1,0:T(8,128)(2,1)S(1)} %collective-permute-done.25.refs_1_) | copy-start | bytes 1179652
  35.3 16.2 %collective-permute-start.26 = (bf16[96,2048]{1,0:T(8,128)(2,1)S(1)}, bf16[96,2048]{1,0:T(8,128)(2,1)S(1)}, u32[]{:S(2)}, u32[]{:S(2)}) collective-permute-start(bf16[96,2048]{1,0:T(8,128)(2,1)S(1)} %collective-permute-done.25.refs_1_), channel_id=1, source_target_pairs={{2,4},{4,6},{6,8},{8,10},{10,12},{12,14},{3,1},{5,3},{7,5},{9,7},{... | collective-permute-start | bytes 1179656 | tf_op jit(solution)/shard_map/ppermute | solution.py:136
  37.2 11.6 %copy-start.20 = (bf16[96,2048]{1,0:T(8,128)(2,1)}, bf16[96,2048]{1,0:T(8,128)(2,1)S(1)}, u32[]{:S(2)}) copy-start(bf16[96,2048]{1,0:T(8,128)(2,1)S(1)} %collective-permute-done.29.refs_1_) | copy-start | bytes 1179652
  37.2 16.2 %collective-permute-start.30 = (bf16[96,2048]{1,0:T(8,128)(2,1)S(1)}, bf16[96,2048]{1,0:T(8,128)(2,1)S(1)}, u32[]{:S(2)}, u32[]{:S(2)}) collective-permute-start(bf16[96,2048]{1,0:T(8,128)(2,1)S(1)} %collective-permute-done.29.refs_1_), channel_id=1, source_target_pairs={{2,0},{4,2},{6,4},{8,6},{10,8},{12,10},{3,5},{5,7},{7,9},{9,11},{1... | collective-permute-start | bytes 1179656 | tf_op jit(solution)/shard_map/ppermute | solution.py:136
  43.1 5.8 %copy-start.16 = (bf16[96,2048]{1,0:T(8,128)(2,1)}, bf16[96,2048]{1,0:T(8,128)(2,1)S(1)}, u32[]{:S(2)}) copy-start(bf16[96,2048]{1,0:T(8,128)(2,1)S(1)} %collective-permute-done.16.refs_0_) | copy-start | bytes 1179652
  43.1 17.1 %collective-permute-start.17 = (bf16[96,2048]{1,0:T(8,128)(2,1)S(1)}, bf16[96,2048]{1,0:T(8,128)(2,1)}, u32[]{:S(2)}, u32[]{:S(2)}) collective-permute-start(bf16[96,2048]{1,0:T(8,128)(2,1)S(1)} %collective-permute-done.16.refs_0_), channel_id=1, source_target_pairs={{6,8},{8,10},{10,12},{12,14},{3,1},{5,3},{7,5},{9,7},{22,24},{24,2... | collective-permute-start | bytes 1179656 | tf_op jit(solution)/shard_map/ppermute | solution.py:136
  45.0 3.8 %copy-start.14 = (bf16[96,2048]{1,0:T(8,128)(2,1)}, bf16[96,2048]{1,0:T(8,128)(2,1)S(1)}, u32[]{:S(2)}) copy-start(bf16[96,2048]{1,0:T(8,128)(2,1)S(1)} %collective-permute-done.20.refs_0_) | copy-start | bytes 1179652
  45.0 15.2 %collective-permute-start.21 = (bf16[96,2048]{1,0:T(8,128)(2,1)S(1)}, bf16[96,2048]{1,0:T(8,128)(2,1)}, u32[]{:S(2)}, u32[]{:S(2)}) collective-permute-start(bf16[96,2048]{1,0:T(8,128)(2,1)S(1)} %collective-permute-done.20.refs_0_), channel_id=1, source_target_pairs={{2,0},{4,2},{6,4},{8,6},{7,9},{9,11},{11,13},{13,15},{18,16},{20,1... | collective-permute-start | bytes 1179656 | tf_op jit(solution)/shard_map/ppermute | solution.py:136
  51.5 9.8 %copy-start.26 = (bf16[96,2048]{1,0:T(8,128)(2,1)}, bf16[96,2048]{1,0:T(8,128)(2,1)S(1)}, u32[]{:S(2)}) copy-start(bf16[96,2048]{1,0:T(8,128)(2,1)S(1)} %collective-permute-done.26.refs_1_) | copy-start | bytes 1179652
  51.5 22.6 %collective-permute-start.27 = (bf16[96,2048]{1,0:T(8,128)(2,1)S(1)}, bf16[96,2048]{1,0:T(8,128)(2,1)S(1)}, u32[]{:S(2)}, u32[]{:S(2)}) collective-permute-start(bf16[96,2048]{1,0:T(8,128)(2,1)S(1)} %collective-permute-done.26.refs_1_), channel_id=1, source_target_pairs={{4,6},{6,8},{8,10},{10,12},{12,14},{3,1},{5,3},{7,5},{9,7},{11,9},... | collective-permute-start | bytes 1179656 | tf_op jit(solution)/shard_map/ppermute | solution.py:136
  53.4 7.9 %copy-start.24 = (bf16[96,2048]{1,0:T(8,128)(2,1)}, bf16[96,2048]{1,0:T(8,128)(2,1)S(1)}, u32[]{:S(2)}) copy-start(bf16[96,2048]{1,0:T(8,128)(2,1)S(1)} %collective-permute-done.30.refs_1_) | copy-start | bytes 1179652
  53.5 22.9 %collective-permute-start.31 = (bf16[96,2048]{1,0:T(8,128)(2,1)S(1)}, bf16[96,2048]{1,0:T(8,128)(2,1)S(1)}, u32[]{:S(2)}, u32[]{:S(2)}) collective-permute-start(bf16[96,2048]{1,0:T(8,128)(2,1)S(1)} %collective-permute-done.30.refs_1_), channel_id=1, source_target_pairs={{2,0},{4,2},{6,4},{8,6},{10,8},{5,7},{7,9},{9,11},{11,13},{13,15},... | collective-permute-start | bytes 1179656 | tf_op jit(solution)/shard_map/ppermute | solution.py:136
  61.3 24.7 %copy-start.4 = (bf16[96,2048]{1,0:T(8,128)(2,1)}, bf16[96,2048]{1,0:T(8,128)(2,1)S(1)}, u32[]{:S(2)}) copy-start(bf16[96,2048]{1,0:T(8,128)(2,1)S(1)} %broadcast_select_fusion.1.refs_0_) | copy-start | bytes 1179652
  61.3 82.5 %all-to-all-start = ((bf16[8,192,256]{2,1,0:T(8,128)(2,1)}), bf16[8,192,256]{2,1,0:T(8,128)(2,1)S(1)}, u32[]{:S(2)}, u32[]{:S(2)}) async-start(bf16[8,192,256]{2,1,0:T(8,128)(2,1)} %bitcast.72), calls=%async_computation | async-start | bytes 1572864 | tf_op jit(solution)/shard_map/all_to_all | solution.py:140
  74.1 38.9 %copy-start.30 = (bf16[96,2048]{1,0:T(8,128)(2,1)}, bf16[96,2048]{1,0:T(8,128)(2,1)S(1)}, u32[]{:S(2)}) copy-start(bf16[96,2048]{1,0:T(8,128)(2,1)S(1)} %collective-permute-done.27.refs_1_) | copy-start | bytes 1179652
  74.1 38.9 %collective-permute-start.28 = (bf16[96,2048]{1,0:T(8,128)(2,1)S(1)}, bf16[96,2048]{1,0:T(8,128)(2,1)S(1)}, u32[]{:S(2)}, u32[]{:S(2)}) collective-permute-start(bf16[96,2048]{1,0:T(8,128)(2,1)S(1)} %collective-permute-done.27.refs_1_), channel_id=1, source_target_pairs={{6,8},{8,10},{10,12},{12,14},{3,1},{5,3},{7,5},{9,7},{22,24},{24,2... | collective-permute-start | bytes 1179656 | tf_op jit(solution)/shard_map/ppermute | solution.py:136
  76.4 36.7 %copy-start.28 = (bf16[96,2048]{1,0:T(8,128)(2,1)}, bf16[96,2048]{1,0:T(8,128)(2,1)S(1)}, u32[]{:S(2)}) copy-start(bf16[96,2048]{1,0:T(8,128)(2,1)S(1)} %collective-permute-done.31.refs_1_) | copy-start | bytes 1179652
  76.4 36.7 %collective-permute-start.32 = (bf16[96,2048]{1,0:T(8,128)(2,1)S(1)}, bf16[96,2048]{1,0:T(8,128)(2,1)S(1)}, u32[]{:S(2)}, u32[]{:S(2)}) collective-permute-start(bf16[96,2048]{1,0:T(8,128)(2,1)S(1)} %collective-permute-done.31.refs_1_), channel_id=1, source_target_pairs={{2,0},{4,2},{6,4},{8,6},{7,9},{9,11},{11,13},{13,15},{18,16},{20,1... | collective-permute-start | bytes 1179656 | tf_op jit(solution)/shard_map/ppermute | solution.py:136
  79.1 63.4 %collective-permute-start.36 = (bf16[2048,128]{1,0:T(8,128)(2,1)}, bf16[2048,128]{1,0:T(8,128)(2,1)}, u32[]{:S(2)}, u32[]{:S(2)}) collective-permute-start(bf16[2048,128]{1,0:T(8,128)(2,1)} %bitcast_convert_fusion), channel_id=1, source_target_pairs={{0,1},{1,0},{2,3},{3,2},{4,5},{5,4},{6,7},{7,6},{8,9},{9,8},{10,11... | collective-permute-start | bytes 1572872 | tf_op jit(solution)/shard_map/ppermute | solution.py:121
  86.0 36.4 %collective-permute-start.22 = (bf16[96,2048]{1,0:T(8,128)(2,1)S(1)}, bf16[96,2048]{1,0:T(8,128)(2,1)S(1)}, u32[]{:S(2)}, u32[]{:S(2)}) collective-permute-start(bf16[96,2048]{1,0:T(8,128)(2,1)S(1)} %broadcast_select_fusion.1.refs_0_), channel_id=1, source_target_pairs={{2,0},{3,1},{4,2},{5,3},{6,4},{7,5},{8,10},{9,11},{10,12},{11,13},... | collective-permute-start | bytes 1179656 | tf_op jit(solution)/shard_map/ppermute | solution.py:136
  113.1 17.7 %collective-permute-start.33 = (bf16[96,2048]{1,0:T(8,128)(2,1)S(1)}, bf16[96,2048]{1,0:T(8,128)(2,1)S(1)}, u32[]{:S(2)}, u32[]{:S(2)}) collective-permute-start(bf16[96,2048]{1,0:T(8,128)(2,1)S(1)} %broadcast_select_fusion.refs_1_), channel_id=1, source_target_pairs={{2,0},{3,1},{4,2},{5,3},{6,4},{7,5},{8,10},{9,11},{10,12},{11,13},... | collective-permute-start | bytes 1179656 | tf_op jit(solution)/shard_map/ppermute | solution.py:136
  122.4 21.5 %copy-start.32 = (bf16[96,2048]{1,0:T(8,128)(2,1)}, bf16[96,2048]{1,0:T(8,128)(2,1)S(1)}, u32[]{:S(2)}) copy-start(bf16[96,2048]{1,0:T(8,128)(2,1)S(1)} %collective-permute-done.22.refs_0_) | copy-start | bytes 1179652
  122.4 12.1 %collective-permute-start.23 = (bf16[96,2048]{1,0:T(8,128)(2,1)S(1)}, bf16[96,2048]{1,0:T(8,128)(2,1)}, u32[]{:S(2)}, u32[]{:S(2)}) collective-permute-start(bf16[96,2048]{1,0:T(8,128)(2,1)S(1)} %collective-permute-done.22.refs_0_), channel_id=1, source_target_pairs={{2,0},{3,1},{4,2},{5,3},{10,12},{11,13},{12,14},{13,15},{18,16},{1... | collective-permute-start | bytes 1179656 | tf_op jit(solution)/shard_map/ppermute | solution.py:136
  130.8 10.3 %collective-permute-start.34 = (bf16[96,2048]{1,0:T(8,128)(2,1)S(1)}, bf16[96,2048]{1,0:T(8,128)(2,1)}, u32[]{:S(2)}, u32[]{:S(2)}) collective-permute-start(bf16[96,2048]{1,0:T(8,128)(2,1)S(1)} %collective-permute-done.33.refs_1_), channel_id=1, source_target_pairs={{2,0},{3,1},{4,2},{5,3},{10,12},{11,13},{12,14},{13,15},{18,16},{1... | collective-permute-start | bytes 1179656 | tf_op jit(solution)/shard_map/ppermute | solution.py:136
  134.4 30.3 %collective-permute-start.24 = (bf16[96,2048]{1,0:T(8,128)(2,1)}, bf16[96,2048]{1,0:T(8,128)(2,1)}, u32[]{:S(2)}, u32[]{:S(2)}) collective-permute-start(bf16[96,2048]{1,0:T(8,128)(2,1)} %collective-permute-done.23.refs_0_), channel_id=1, source_target_pairs={{2,0},{3,1},{12,14},{13,15},{18,16},{19,17},{28,30},{29,31},{34,32... | collective-permute-start | bytes 1179656 | tf_op jit(solution)/shard_map/ppermute | solution.py:136
  141.1 23.7 %collective-permute-start.35 = (bf16[96,2048]{1,0:T(8,128)(2,1)}, bf16[96,2048]{1,0:T(8,128)(2,1)}, u32[]{:S(2)}, u32[]{:S(2)}) collective-permute-start(bf16[96,2048]{1,0:T(8,128)(2,1)} %collective-permute-done.34.refs_1_), channel_id=1, source_target_pairs={{2,0},{3,1},{12,14},{13,15},{18,16},{19,17},{28,30},{29,31},{34,32... | collective-permute-start | bytes 1179656 | tf_op jit(solution)/shard_map/ppermute | solution.py:136
  148.0 2.0 copy-start.13
  148.0 2.0 copy-start.21
  148.0 2.0 copy-start.36
  150.1 2.0 copy-start.11
  150.1 2.0 copy-start.27
  150.1 2.0 copy-start.42
  152.1 2.0 copy-start.9
  154.2 2.0 copy-start.17
  154.2 2.0 copy-start.31
  154.2 2.0 copy-start.37
  159.4 2.2 copy-start.33
  159.4 2.2 copy-start.35
  165.9 7.5 %collective-permute-start.37 = (f32[2048,128]{1,0:T(8,128)S(1)}, f32[2048,128]{1,0:T(8,128)}, u32[]{:S(2)}, u32[]{:S(2)}) collective-permute-start(f32[2048,128]{1,0:T(8,128)S(1)} %get-tuple-element.67), channel_id=1, source_target_pairs={{0,1},{1,0},{2,3},{3,2},{4,5},{5,4},{6,7},{7,6},{8,9},{9,8},{10,11... | collective-permute-start | bytes 3145736 | tf_op jit(solution)/shard_map/ppermute | solution.py:171
  176.3 58.1 %collective-permute-start = (bf16[2048,128]{1,0:T(8,128)(2,1)S(1)}, bf16[2048,128]{1,0:T(8,128)(2,1)}, u32[]{:S(2)}, u32[]{:S(2)}) collective-permute-start(bf16[2048,128]{1,0:T(8,128)(2,1)S(1)} %param.2), channel_id=1, source_target_pairs={{0,64},{16,80},{32,96},{48,112},{64,128},{80,144},{96,160},{112,17... | collective-permute-start | bytes 1572872 | tf_op jit(solution)/shard_map/cond/branch_2_fun/ppermute | solution.py:76
  (21 other events, 26.7 us)
